TPU v7x, 512 devices: a whole 4x4x16 slice. The times are simulated.
512 devices in a mesh: block: 64 (over y_lo, z, core), view: 8 (over y_hi, x).
Axes of the slice: x: 4, y: 4 (y_hi: 2, y_lo: 2; y = y_hi * 2 + y_lo), z: 16, core: 2. Of those that a mesh axis runs over, the one named last changes fastest.
Arguments:
- estimate: float32 [64, 32, 48, 128], P('block'), may hold values from 0.5 to 2
- views_data: float32 [8, 64, 32, 48, 128], P('view', 'block'), may hold values from 0.1 to 10
- psf_taps: float32 [8, 3, 31], P('view'), may hold values from 0.05 to 1
- view_bounds: int32 [8, 4], replicated, may hold values from 0 to 512, as said below
Outputs:
- joined: float32 [64, 32, 48, 128], P('block')
Inputs may be any that keep to these rules, and one draw needn't show every extreme that they name: `view_bounds`: for each view start < end along z and y, ends at most 512 along z and 192 along y; one view covers the whole grid.
All inputs are finite; a program needn't handle non-finite values.
Results may differ from a plain program's by a relative error of at most 0.0001.
Values sent between devices are 32-bit elements; how exact they have to be, the bound alone decides.
A program may use at most 192 MiB of HBM per device.

v0:
```python
import jax
import jax.numpy as jnp
from jax import lax
from jax.sharding import PartitionSpec as P

BY = 4
ITERS = 2


def from_behind(value, axis, steps):
    count = lax.axis_size(axis)
    first, last = (max(0, -steps), min(count, count - steps))
    return lax.ppermute(value, axis, [(source, source + steps) for source in range(first, last)])


def pad_depth(field, half):
    below = from_behind(field[-half:], "block", BY)
    above = from_behind(field[:half], "block", -BY)
    return jnp.concatenate([below, field, above], axis=0)


def pad_sides(field, half, column):
    below = from_behind(field[:, -half:], "block", 1)
    above = from_behind(field[:, :half], "block", -1)
    below = jnp.where(column > 0, below, jnp.zeros_like(below))
    above = jnp.where(column < BY - 1, above, jnp.zeros_like(above))
    return jnp.concatenate([below, field, above], axis=1)


def band_matrix(taps, width, half):
    rows = jnp.arange(width, dtype=jnp.int32)[:, None]
    cols = jnp.arange(width, dtype=jnp.int32)[None, :]
    offset = rows - cols + half
    matrix = jnp.zeros((width, width), jnp.float32)
    for tap in range(taps.shape[0]):
        matrix = matrix + jnp.where(offset == tap, taps[tap], 0.0)
    return matrix


def along_x(field, matrix):
    flat = field.reshape(-1, field.shape[-1])
    out = jnp.dot(flat, matrix, precision=lax.Precision.HIGHEST, preferred_element_type=jnp.float32)
    return out.reshape(field.shape)


def tap_sum(extended, taps, length, axis):
    total = jnp.zeros(extended.shape[:axis] + (length,) + extended.shape[axis + 1 :], jnp.float32)
    for tap in range(taps.shape[0]):
        total = total + taps[tap] * lax.slice_in_dim(extended, tap, tap + length, axis=axis)
    return total


def blur(field, taps, matrix, half, column):
    depth, height = (field.shape[0], field.shape[1])
    filtered = along_x(field, matrix)
    filtered = tap_sum(pad_depth(filtered, half), taps[0], depth, 0)
    return tap_sum(pad_sides(filtered, half, column), taps[1], height, 1)


def view_sum(logs):
    return lax.psum(logs, "view")


def body(estimate, views_data, psf_taps, view_bounds):
    volume = estimate[0]
    depth, height, width = volume.shape
    half = psf_taps.shape[2] // 2
    place = lax.axis_index("block")
    row_index = place // BY
    column = place % BY
    zpos = row_index * depth + jnp.arange(depth, dtype=jnp.int32)[:, None]
    ypos = column * height + jnp.arange(height, dtype=jnp.int32)[None, :]
    lower_z = view_bounds[:, 0][:, None, None]
    upper_z = view_bounds[:, 1][:, None, None]
    lower_y = view_bounds[:, 2][:, None, None]
    upper_y = view_bounds[:, 3][:, None, None]
    inside = (
        (zpos[None] >= lower_z)
        & (zpos[None] < upper_z)
        & (ypos[None] >= lower_y)
        & (ypos[None] < upper_y)
    )
    masks = inside.astype(jnp.float32)[:, :, :, None]
    count = jnp.sum(masks, axis=0)
    held = psf_taps.shape[0]
    first_view = lax.axis_index("view") * held
    own_masks = lax.dynamic_slice_in_dim(masks, first_view, held, 0)
    normed = psf_taps / jnp.sum(psf_taps, axis=2, keepdims=True)
    forward = band_matrix(normed[0, 2], width, half)
    flipped = band_matrix(normed[0, 2, ::-1], width, half)
    for step in range(ITERS):
        taps = normed[0]
        blurred = blur(volume, taps, forward, half, column)
        ratio = views_data[0, 0] / blurred
        correction = blur(ratio, taps[:, ::-1], flipped, half, column)
        logs = own_masks[0] * jnp.log(correction)
        total = view_sum(logs)
        volume = volume * jnp.exp(total / count)
    return volume[None]


def solution(mesh):
    return jax.shard_map(
        body,
        mesh=mesh,
        in_specs=(
            P("block", None, None, None),
            P("view", "block", None, None, None),
            P("view", None, None),
            P(),
        ),
        out_specs=P("block", None, None, None),
        check_vma=False,
    )
```

profile of v0, /device:TPU:1, one launch (start us, length us, event | category | flops | bytes accessed | tf_op | source)
XLA Modules:
  0.0 624.4 jit_solution(6080823266023669805)
XLA Ops:
  9.5 21.5 %convolution_bitcast_fusion = f32[1536,128]{0,1:T(8,128)S(1)} fusion(f32[1536,128]{1,0:T(8,128)} %bitcast.203, f32[]{:T(128)} %bitcast.43, f32[]{:T(128)} %bitcast.42, f32[]{:T(128)} %bitcast.41, f32[]{:T(128)} %bitcast.40, f32[]{:T(128)} %bitcast.39, f32[]{:T(128)} %bitcast.38, f32[]{:T(128)} %bitcast.37, f32[]{:T(128)} %bitcast.36, f32[]{:T(128)} %bitcast.35, ...), kind=kOutput, calls=%fused_computation.336 | convolution fusion | flops 303529984 | bytes 1572988 | tf_op jit(solution)/shard_map/dot_general | solution.py:42
  32.8 6.4 %collective-permute-start = (f32[15,48,128]{2,1,0:T(8,128)S(1)}, f32[15,48,128]{2,1,0:T(8,128)S(1)}, u32[]{:S(2)}, u32[]{:S(2)}) collective-permute-start(f32[15,48,128]{2,1,0:T(8,128)S(1)} %bitcast.207), channel_id=1, source_target_pairs={{0,32},{8,40},{16,48},{24,56},{32,64},{40,72},{48,80},{56,88},{64,... | collective-permute-start | bytes 1105928 | tf_op jit(solution)/shard_map/ppermute | solution.py:13
  41.1 8.6 %collective-permute-done.1 = f32[15,48,128]{2,1,0:T(8,128)S(1)} collective-permute-done((f32[15,48,128]{2,1,0:T(8,128)S(1)}, f32[15,48,128]{2,1,0:T(8,128)S(1)}, u32[]{:S(2)}, u32[]{:S(2)}) %collective-permute-start.1) | collective-permute-done | bytes 368672 | tf_op jit(solution)/shard_map/ppermute | solution.py:13
  49.8 21.4 %fusion.611 = f32[32,48,128]{2,1,0:T(8,128)S(1)} fusion(f32[32,48,128]{2,1,0:T(8,128)S(1)} %bitcast.198, f32[15,48,128]{2,1,0:T(8,128)S(1)} %collective-permute-done.1, f32[15,48,128]{2,1,0:T(8,128)S(1)} %collective-permute-done, f32[]{:T(128)} %bitcast.78, f32[]{:T(128)} %bitcast.77, f32[]{:T(128)} %bitcast.76, f32[]{:T(128)} %bitcast.75, f32[]{:T(128)} %bitcast.74, ...), kind=kLoop, calls=%fused_computation.1060 | loop fusion | flops 17891328 | bytes 2310268 | tf_op jit(solution)/shard_map/add | solution.py:49
  71.2 9.3 %collective-permute-start.2 = (f32[32,15,128]{2,1,0:T(8,128)S(1)}, f32[32,15,128]{2,1,0:T(8,128)S(1)}, u32[]{:S(2)}, u32[]{:S(2)}) collective-permute-start(f32[32,15,128]{2,1,0:T(8,128)S(1)} %get-tuple-element.17), channel_id=1, source_target_pairs={{0,8},{8,16},{16,24},{24,32},{32,40},{40,48},{48,56},{56,64},{64,7... | collective-permute-start | bytes 737288 | tf_op jit(solution)/shard_map/ppermute | solution.py:13
  88.3 23.0 %fusion.267 = f32[32,48,128]{2,1,0:T(8,128)S(1)} fusion(f32[32,48,128]{2,1,0:T(8,128)S(1)} %fusion.611, f32[32,15,128]{2,1,0:T(8,128)S(1)} %broadcast_select_fusion.6, f32[32,15,128]{2,1,0:T(8,128)S(1)} %broadcast_select_fusion.7, f32[1,1,32,48,128]{4,3,2,1,0:T(8,128)S(1)} %copy-done, f32[]{:T(128)} %bitcast.108, f32[]{:T(128)} %bitcast.107, f32[]{:T(128)} %bitcast.106, ...), kind=kLoop, calls=%fused_computation.716 | loop fusion | flops 18087936 | bytes 2850940 | tf_op jit(solution)/shard_map/div | solution.py:94
  111.3 20.2 %fusion.773 = f32[1536,128]{1,0:T(8,128)S(1)} fusion(f32[1536,128]{1,0:T(8,128)S(1)} %bitcast.205, f32[]{:T(128)} %bitcast.43, f32[]{:T(128)} %bitcast.42, f32[]{:T(128)} %bitcast.41, f32[]{:T(128)} %bitcast.40, f32[]{:T(128)} %bitcast.39, f32[]{:T(128)} %bitcast.38, f32[]{:T(128)} %bitcast.37, f32[]{:T(128)} %bitcast.36, f32[]{:T(128)} %bitcast.35, ...), kind=kOutput, calls=%fused_computation.1251 | convolution fusion | flops 303529984 | bytes 1572988 | tf_op jit(solution)/shard_map/dot_general | solution.py:42
  132.8 5.7 collective-permute-start.4
  140.0 13.4 %collective-permute-done.5 = f32[15,48,128]{2,1,0:T(8,128)S(1)} collective-permute-done((f32[15,48,128]{2,1,0:T(8,128)S(1)}, f32[15,48,128]{2,1,0:T(8,128)S(1)}, u32[]{:S(2)}, u32[]{:S(2)}) %collective-permute-start.5) | collective-permute-done | bytes 368672 | tf_op jit(solution)/shard_map/ppermute | solution.py:13
  153.4 21.8 %fusion.525 = f32[32,48,128]{2,1,0:T(8,128)S(1)} fusion(f32[32,48,128]{2,1,0:T(8,128)S(1)} %bitcast.201, f32[15,48,128]{2,1,0:T(8,128)S(1)} %collective-permute-done.5, f32[15,48,128]{2,1,0:T(8,128)S(1)} %collective-permute-done.4, f32[]{:T(128)} %bitcast.142, f32[]{:T(128)} %bitcast.141, f32[]{:T(128)} %bitcast.140, f32[]{:T(128)} %bitcast.139, ...), kind=kLoop, calls=%fused_computation.974 | loop fusion | flops 17891328 | bytes 2310268 | tf_op jit(solution)/shard_map/add | solution.py:49
  182.2 5.0 collective-permute-done.7
  187.3 24.0 %fusion.180 = f32[32,48,128]{2,1,0:T(8,128)} fusion(f32[32,48,128]{2,1,0:T(8,128)S(1)} %fusion.525, f32[32,15,128]{2,1,0:T(8,128)S(1)} %broadcast_select_fusion.4, f32[32,15,128]{2,1,0:T(8,128)S(1)} %broadcast_select_fusion.5, f32[]{:T(128)} %bitcast.172, f32[]{:T(128)} %bitcast.171, f32[]{:T(128)} %bitcast.170, f32[]{:T(128)} %bitcast.169, f32[]{:T(128)} %bitcast.168, ...), kind=kLoop, calls=%fused_computation.629 | loop fusion | flops 18087936 | bytes 2070652 | tf_op jit(solution)/shard_map/mul | solution.py:96
  211.5 105.3 %all-reduce.3.cloned.1.call-done = f32[32,48,128]{2,1,0:T(8,128)} async-done(((f32[32,48,128]{2,1,0:T(8,128)}), f32[32,48,128]{2,1,0:T(8,128)}) %all-reduce.3.cloned.1.call-update) | async-done | bytes 786448 | tf_op jit(solution)/shard_map/psum | solution.py:61
  318.2 20.2 %fusion.775 = f32[1536,128]{1,0:T(8,128)S(1)} fusion(f32[1536,128]{1,0:T(8,128)S(1)} %bitcast.199, f32[]{:T(128)} %bitcast.43, f32[]{:T(128)} %bitcast.42, f32[]{:T(128)} %bitcast.41, f32[]{:T(128)} %bitcast.40, f32[]{:T(128)} %bitcast.39, f32[]{:T(128)} %bitcast.38, f32[]{:T(128)} %bitcast.37, f32[]{:T(128)} %bitcast.36, f32[]{:T(128)} %bitcast.35, ...), kind=kOutput, calls=%fused_computation.1252 | convolution fusion | flops 303529984 | bytes 1572988 | tf_op jit(solution)/shard_map/dot_general | solution.py:42
  344.7 11.8 %collective-permute-done.9 = f32[15,48,128]{2,1,0:T(8,128)S(1)} collective-permute-done((f32[15,48,128]{2,1,0:T(8,128)S(1)}, f32[15,48,128]{2,1,0:T(8,128)S(1)}, u32[]{:S(2)}, u32[]{:S(2)}) %collective-permute-start.9) | collective-permute-done | bytes 368672 | tf_op jit(solution)/shard_map/ppermute | solution.py:13
  356.4 21.6 %fusion.439 = f32[32,48,128]{2,1,0:T(8,128)S(1)} fusion(f32[32,48,128]{2,1,0:T(8,128)S(1)} %bitcast.202, f32[15,48,128]{2,1,0:T(8,128)S(1)} %collective-permute-done.9, f32[15,48,128]{2,1,0:T(8,128)S(1)} %collective-permute-done.8, f32[]{:T(128)} %bitcast.78, f32[]{:T(128)} %bitcast.77, f32[]{:T(128)} %bitcast.76, f32[]{:T(128)} %bitcast.75, f32[]{:T(128)} %bitcast.74, ...), kind=kLoop, calls=%fused_computation.888 | loop fusion | flops 17891328 | bytes 2310268 | tf_op jit(solution)/shard_map/add | solution.py:49
  378.1 8.0 %collective-permute-start.10 = (f32[32,15,128]{2,1,0:T(8,128)S(1)}, f32[32,15,128]{2,1,0:T(8,128)S(1)}, u32[]{:S(2)}, u32[]{:S(2)}) collective-permute-start(f32[32,15,128]{2,1,0:T(8,128)S(1)} %get-tuple-element.9), channel_id=1, source_target_pairs={{0,8},{8,16},{16,24},{24,32},{32,40},{40,48},{48,56},{56,64},{64,7... | collective-permute-start | bytes 737288 | tf_op jit(solution)/shard_map/ppermute | solution.py:13
  393.8 23.0 %fusion.92 = f32[32,48,128]{2,1,0:T(8,128)S(1)} fusion(f32[32,48,128]{2,1,0:T(8,128)S(1)} %fusion.439, f32[32,15,128]{2,1,0:T(8,128)S(1)} %broadcast_select_fusion.2, f32[32,15,128]{2,1,0:T(8,128)S(1)} %broadcast_select_fusion.3, f32[1,1,32,48,128]{4,3,2,1,0:T(8,128)S(1)} %copy-done, f32[]{:T(128)} %bitcast.108, f32[]{:T(128)} %bitcast.107, f32[]{:T(128)} %bitcast.106, ...), kind=kLoop, calls=%fused_computation.541 | loop fusion | flops 18087936 | bytes 2850940 | tf_op jit(solution)/shard_map/div | solution.py:94
  416.8 20.2 %fusion.771 = f32[1536,128]{1,0:T(8,128)S(1)} fusion(f32[1536,128]{1,0:T(8,128)S(1)} %bitcast.204, f32[]{:T(128)} %bitcast.43, f32[]{:T(128)} %bitcast.42, f32[]{:T(128)} %bitcast.41, f32[]{:T(128)} %bitcast.40, f32[]{:T(128)} %bitcast.39, f32[]{:T(128)} %bitcast.38, f32[]{:T(128)} %bitcast.37, f32[]{:T(128)} %bitcast.36, f32[]{:T(128)} %bitcast.35, ...), kind=kOutput, calls=%fused_computation.1250 | convolution fusion | flops 303529984 | bytes 1572988 | tf_op jit(solution)/shard_map/dot_general | solution.py:42
  438.4 5.7 collective-permute-start.12
  444.1 14.0 %collective-permute-done.13 = f32[15,48,128]{2,1,0:T(8,128)S(1)} collective-permute-done((f32[15,48,128]{2,1,0:T(8,128)S(1)}, f32[15,48,128]{2,1,0:T(8,128)S(1)}, u32[]{:S(2)}, u32[]{:S(2)}) %collective-permute-start.13) | collective-permute-done | bytes 368672 | tf_op jit(solution)/shard_map/ppermute | solution.py:13
  458.1 21.9 %fusion.353 = f32[32,48,128]{2,1,0:T(8,128)S(1)} fusion(f32[32,48,128]{2,1,0:T(8,128)S(1)} %bitcast.200, f32[15,48,128]{2,1,0:T(8,128)S(1)} %collective-permute-done.13, f32[15,48,128]{2,1,0:T(8,128)S(1)} %collective-permute-done.12, f32[]{:T(128)} %bitcast.142, f32[]{:T(128)} %bitcast.141, f32[]{:T(128)} %bitcast.140, f32[]{:T(128)} %bitcast.139, ...), kind=kLoop, calls=%fused_computation.802 | loop fusion | flops 17891328 | bytes 2310268 | tf_op jit(solution)/shard_map/add | solution.py:49
  492.3 24.0 %fusion.5 = f32[32,48,128]{2,1,0:T(8,128)} fusion(f32[32,48,128]{2,1,0:T(8,128)S(1)} %fusion.353, f32[32,15,128]{2,1,0:T(8,128)S(1)} %broadcast_select_fusion, f32[32,15,128]{2,1,0:T(8,128)S(1)} %broadcast_select_fusion.1, f32[]{:T(128)} %bitcast.172, f32[]{:T(128)} %bitcast.171, f32[]{:T(128)} %bitcast.170, f32[]{:T(128)} %bitcast.169, f32[]{:T(128)} %bitcast.168, ...), kind=kLoop, calls=%fused_computation.454 | loop fusion | flops 18087936 | bytes 2070652 | tf_op jit(solution)/shard_map/mul | solution.py:96
  516.4 98.9 %all-reduce.5.cloned.1.call-done = f32[32,48,128]{2,1,0:T(8,128)} async-done(((f32[32,48,128]{2,1,0:T(8,128)}), f32[32,48,128]{2,1,0:T(8,128)}) %all-reduce.5.cloned.1.call-update) | async-done | bytes 786448 | tf_op jit(solution)/shard_map/psum | solution.py:61
  (74 shorter events, 55.8 us)
Async XLA Ops:
  6.5 310.2 %all-reduce.3.cloned.1.call-start = ((), (), s32[]{:S(2)}) async-start(), calls=%async_computation | async-start | bytes 1572864 | tf_op jit(solution)/shard_map/psum | solution.py:61
  31.2 8.8 %copy-start.2 = (s32[8,4]{0,1:T(4,128)S(1)}, s32[8,4]{0,1:T(4,128)}, u32[]{:S(2)}) copy-start(s32[8,4]{0,1:T(4,128)} %param.7) | copy-start | bytes 388
  31.3 18.4 %collective-permute-start.1 = (f32[15,48,128]{2,1,0:T(8,128)S(1)}, f32[15,48,128]{2,1,0:T(8,128)S(1)}, u32[]{:S(2)}, u32[]{:S(2)}) collective-permute-start(f32[15,48,128]{2,1,0:T(8,128)S(1)} %bitcast.206), channel_id=1, source_target_pairs={{32,0},{40,8},{48,16},{56,24},{64,32},{72,40},{80,48},{88,56},{96,... | collective-permute-start | bytes 1105928 | tf_op jit(solution)/shard_map/ppermute | solution.py:13
  32.8 17.0 %collective-permute-start = (f32[15,48,128]{2,1,0:T(8,128)S(1)}, f32[15,48,128]{2,1,0:T(8,128)S(1)}, u32[]{:S(2)}, u32[]{:S(2)}) collective-permute-start(f32[15,48,128]{2,1,0:T(8,128)S(1)} %bitcast.207), channel_id=1, source_target_pairs={{0,32},{8,40},{16,48},{24,56},{32,64},{40,72},{48,80},{56,88},{64,... | collective-permute-start | bytes 1105928 | tf_op jit(solution)/shard_map/ppermute | solution.py:13
  71.2 17.0 %copy-start = (f32[1,1,32,48,128]{4,3,2,1,0:T(8,128)S(1)}, f32[1,1,32,48,128]{4,3,2,1,0:T(8,128)}, u32[]{:S(2)}) copy-start(f32[1,1,32,48,128]{4,3,2,1,0:T(8,128)} %param.5) | copy-start | bytes 2359300
  71.2 12.6 %collective-permute-start.2 = (f32[32,15,128]{2,1,0:T(8,128)S(1)}, f32[32,15,128]{2,1,0:T(8,128)S(1)}, u32[]{:S(2)}, u32[]{:S(2)}) collective-permute-start(f32[32,15,128]{2,1,0:T(8,128)S(1)} %get-tuple-element.17), channel_id=1, source_target_pairs={{0,8},{8,16},{16,24},{24,32},{32,40},{40,48},{48,56},{56,64},{64,7... | collective-permute-start | bytes 737288 | tf_op jit(solution)/shard_map/ppermute | solution.py:13
  80.5 7.7 %collective-permute-start.3 = (f32[32,15,128]{2,1,0:T(8,128)S(1)}, f32[32,15,128]{2,1,0:T(8,128)S(1)}, u32[]{:S(2)}, u32[]{:S(2)}) collective-permute-start(f32[32,15,128]{2,1,0:T(8,128)S(1)} %get-tuple-element.18), channel_id=1, source_target_pairs={{8,0},{16,8},{24,16},{32,24},{40,32},{48,40},{56,48},{64,56},{72,6... | collective-permute-start | bytes 737288 | tf_op jit(solution)/shard_map/ppermute | solution.py:13
  131.5 21.9 %collective-permute-start.5 = (f32[15,48,128]{2,1,0:T(8,128)S(1)}, f32[15,48,128]{2,1,0:T(8,128)S(1)}, u32[]{:S(2)}, u32[]{:S(2)}) collective-permute-start(f32[15,48,128]{2,1,0:T(8,128)S(1)} %bitcast.209), channel_id=1, source_target_pairs={{32,0},{40,8},{48,16},{56,24},{64,32},{72,40},{80,48},{88,56},{96,... | collective-permute-start | bytes 1105928 | tf_op jit(solution)/shard_map/ppermute | solution.py:13
  132.8 20.6 %collective-permute-start.4 = (f32[15,48,128]{2,1,0:T(8,128)S(1)}, f32[15,48,128]{2,1,0:T(8,128)S(1)}, u32[]{:S(2)}, u32[]{:S(2)}) collective-permute-start(f32[15,48,128]{2,1,0:T(8,128)S(1)} %bitcast.208), channel_id=1, source_target_pairs={{0,32},{8,40},{16,48},{24,56},{32,64},{40,72},{48,80},{56,88},{64,... | collective-permute-start | bytes 1105928 | tf_op jit(solution)/shard_map/ppermute | solution.py:13
  175.2 7.0 %collective-permute-start.6 = (f32[32,15,128]{2,1,0:T(8,128)S(1)}, f32[32,15,128]{2,1,0:T(8,128)S(1)}, u32[]{:S(2)}, u32[]{:S(2)}) collective-permute-start(f32[32,15,128]{2,1,0:T(8,128)S(1)} %get-tuple-element.13), channel_id=1, source_target_pairs={{0,8},{8,16},{16,24},{24,32},{32,40},{40,48},{48,56},{56,64},{64,7... | collective-permute-start | bytes 737288 | tf_op jit(solution)/shard_map/ppermute | solution.py:13
  179.6 7.7 %collective-permute-start.7 = (f32[32,15,128]{2,1,0:T(8,128)S(1)}, f32[32,15,128]{2,1,0:T(8,128)S(1)}, u32[]{:S(2)}, u32[]{:S(2)}) collective-permute-start(f32[32,15,128]{2,1,0:T(8,128)S(1)} %get-tuple-element.14), channel_id=1, source_target_pairs={{8,0},{16,8},{24,16},{32,24},{40,32},{48,40},{56,48},{64,56},{72,6... | collective-permute-start | bytes 737288 | tf_op jit(solution)/shard_map/ppermute | solution.py:13
  211.3 105.4 %copy-start.1 = (f32[1,32,48,128]{3,2,1,0:T(8,128)S(1)}, f32[1,32,48,128]{3,2,1,0:T(8,128)}, u32[]{:S(2)}) copy-start(f32[1,32,48,128]{3,2,1,0:T(8,128)} %param.4) | copy-start | bytes 2359300
  211.3 404.0 %all-reduce.5.cloned.1.call-start = ((), (), s32[]{:S(2)}) async-start(), calls=%async_computation.1 | async-start | bytes 1572864 | tf_op jit(solution)/shard_map/psum | solution.py:61
  338.4 18.0 %collective-permute-start.9 = (f32[15,48,128]{2,1,0:T(8,128)S(1)}, f32[15,48,128]{2,1,0:T(8,128)S(1)}, u32[]{:S(2)}, u32[]{:S(2)}) collective-permute-start(f32[15,48,128]{2,1,0:T(8,128)S(1)} %bitcast.212), channel_id=1, source_target_pairs={{32,0},{40,8},{48,16},{56,24},{64,32},{72,40},{80,48},{88,56},{96,... | collective-permute-start | bytes 1105928 | tf_op jit(solution)/shard_map/ppermute | solution.py:13
  339.7 16.7 %collective-permute-start.8 = (f32[15,48,128]{2,1,0:T(8,128)S(1)}, f32[15,48,128]{2,1,0:T(8,128)S(1)}, u32[]{:S(2)}, u32[]{:S(2)}) collective-permute-start(f32[15,48,128]{2,1,0:T(8,128)S(1)} %bitcast.210), channel_id=1, source_target_pairs={{0,32},{8,40},{16,48},{24,56},{32,64},{40,72},{48,80},{56,88},{64,... | collective-permute-start | bytes 1105928 | tf_op jit(solution)/shard_map/ppermute | solution.py:13
  378.1 11.3 %collective-permute-start.10 = (f32[32,15,128]{2,1,0:T(8,128)S(1)}, f32[32,15,128]{2,1,0:T(8,128)S(1)}, u32[]{:S(2)}, u32[]{:S(2)}) collective-permute-start(f32[32,15,128]{2,1,0:T(8,128)S(1)} %get-tuple-element.9), channel_id=1, source_target_pairs={{0,8},{8,16},{16,24},{24,32},{32,40},{40,48},{48,56},{56,64},{64,7... | collective-permute-start | bytes 737288 | tf_op jit(solution)/shard_map/ppermute | solution.py:13
  386.1 7.7 %collective-permute-start.11 = (f32[32,15,128]{2,1,0:T(8,128)S(1)}, f32[32,15,128]{2,1,0:T(8,128)S(1)}, u32[]{:S(2)}, u32[]{:S(2)}) collective-permute-start(f32[32,15,128]{2,1,0:T(8,128)S(1)} %get-tuple-element.10), channel_id=1, source_target_pairs={{8,0},{16,8},{24,16},{32,24},{40,32},{48,40},{56,48},{64,56},{72,6... | collective-permute-start | bytes 737288 | tf_op jit(solution)/shard_map/ppermute | solution.py:13
  437.1 21.0 %collective-permute-start.13 = (f32[15,48,128]{2,1,0:T(8,128)S(1)}, f32[15,48,128]{2,1,0:T(8,128)S(1)}, u32[]{:S(2)}, u32[]{:S(2)}) collective-permute-start(f32[15,48,128]{2,1,0:T(8,128)S(1)} %bitcast.213), channel_id=1, source_target_pairs={{32,0},{40,8},{48,16},{56,24},{64,32},{72,40},{80,48},{88,56},{96,... | collective-permute-start | bytes 1105928 | tf_op jit(solution)/shard_map/ppermute | solution.py:13
  438.4 19.7 %collective-permute-start.12 = (f32[15,48,128]{2,1,0:T(8,128)S(1)}, f32[15,48,128]{2,1,0:T(8,128)S(1)}, u32[]{:S(2)}, u32[]{:S(2)}) collective-permute-start(f32[15,48,128]{2,1,0:T(8,128)S(1)} %bitcast.211), channel_id=1, source_target_pairs={{0,32},{8,40},{16,48},{24,56},{32,64},{40,72},{48,80},{56,88},{64,... | collective-permute-start | bytes 1105928 | tf_op jit(solution)/shard_map/ppermute | solution.py:13
  480.0 7.9 %collective-permute-start.14 = (f32[32,15,128]{2,1,0:T(8,128)S(1)}, f32[32,15,128]{2,1,0:T(8,128)S(1)}, u32[]{:S(2)}, u32[]{:S(2)}) collective-permute-start(f32[32,15,128]{2,1,0:T(8,128)S(1)} %get-tuple-element.5), channel_id=1, source_target_pairs={{0,8},{8,16},{16,24},{24,32},{32,40},{40,48},{48,56},{56,64},{64,7... | collective-permute-start | bytes 737288 | tf_op jit(solution)/shard_map/ppermute | solution.py:13
  484.6 7.7 %collective-permute-start.15 = (f32[32,15,128]{2,1,0:T(8,128)S(1)}, f32[32,15,128]{2,1,0:T(8,128)S(1)}, u32[]{:S(2)}, u32[]{:S(2)}) collective-permute-start(f32[32,15,128]{2,1,0:T(8,128)S(1)} %get-tuple-element.6), channel_id=1, source_target_pairs={{8,0},{16,8},{24,16},{32,24},{40,32},{48,40},{56,48},{64,56},{72,6... | collective-permute-start | bytes 737288 | tf_op jit(solution)/shard_map/ppermute | solution.py:13
Sparse Core Ops, SparseCore 0:
  211.4 105.2 all-reduce.2
  516.5 98.7 all-reduce.4
where the time goes:
time: 632 us; the launch traced here: 624 us
  waiting for transfers between devices  273 us (43%)
  other arithmetic  186 us (29%)
  matrix products  82 us (13%)
  starting transfers between devices  61.2 us (10%)
  between operations  13.9 us (2%)
  local copies, waits for them, and re-layouts  7.57 us (1%)
    psum x2, waiting for transfers between devices, view_sum(): return lax.psum(logs, 'view')  204 us
    add x4, other arithmetic, tap_sum(): total + taps[tap] * lax.slice_in_dim(extended, tap, tap + length, axis=axis)  86.7 us
    dot_general x4, matrix products, along_x(): jnp.dot(flat, matrix, precision=lax.Precision.HIGHEST, preferred_element_...  82 us
    ppermute x16, waiting for transfers between devices, from_behind(): lax.ppermute(value, axis, [(source, source + steps) for source in range(f...  69.1 us
    ppermute x16, starting transfers between devices, from_behind(): lax.ppermute(value, axis, [(source, source + steps) for source in range(f...  61.2 us
    mul x3, other arithmetic, body(): logs = own_masks[0] * jnp.log(correction)  48.1 us
    div x2, other arithmetic, body(): ratio = views_data[0, 0] / blurred  46 us
  transfers between devices with their start and end apart: 18, of which 13 were waited for; matrix products, arithmetic and copies ran while one was open for 1% of the time, Pallas kernels for 0%

commit v1 on v0

v1 whole, which is shorter than its diff:
```python
import functools

import jax
import jax.numpy as jnp
from jax import lax
from jax.experimental import pallas as pl
from jax.experimental.pallas import tpu as pltpu
from jax.sharding import PartitionSpec as P

MESH = pl.DeviceIdType.MESH
F32 = jnp.float32
BF16 = jnp.bfloat16

BY = 4
ITERS = 2
Z, Y, X = 32, 48, 128
TAPS = 31
HALF = 15
PAD = 16
VIEW_X, VIEW_Y = 4, 2
VIEWS = VIEW_X * VIEW_Y
PIECE = Z // VIEWS
YC = 16
NJ = Y // YC
ORDER = (0, 2, 1)
ZC = 8
NZC = Z // ZC


def split(x):
    hi = x.astype(BF16)
    lo = (x - hi.astype(F32)).astype(BF16)
    return hi, lo


def fill_tap(offset, taps, flip):
    acc = jnp.zeros(offset.shape, F32)
    for k in range(TAPS):
        at = TAPS - 1 - k if flip else k
        acc = jnp.where(offset == k, taps[:, at : at + 1], acc)
    return acc


def build_matrices(taps, kz_ref, ky_ref, wx_ref):
    tz, ty, tx = taps[0:1], taps[1:2], taps[2:3]
    for f in range(2):

        def z_rows(i, _):
            r0 = pl.multiple_of(i * 16, 16)
            row = lax.broadcasted_iota(jnp.int32, (16, 512), 0) + r0
            col = lax.broadcasted_iota(jnp.int32, (16, 512), 1)
            d = col - row
            k = jnp.where((d & 7) == 0, (d >> 3) - 1, -1)
            hi, lo = split(fill_tap(k, tz, f == 1))
            kz_ref[f, pl.ds(r0, 16), 0:512] = hi
            kz_ref[f, pl.ds(r0, 16), 512:1024] = hi
            kz_ref[f, pl.ds(r0, 16), 1024:1536] = lo
            return 0

        lax.fori_loop(0, 16, z_rows, 0)

        row = lax.broadcasted_iota(jnp.int32, (Y, 256), 0)
        col = lax.broadcasted_iota(jnp.int32, (Y, 256), 1)
        part = jnp.where(col >= 160, 2, jnp.where(col >= 80, 1, 0))
        k = jnp.where(col < 240, col - 80 * part - 1 - row, -1)
        val = fill_tap(k, ty, f == 1)
        hi = val.astype(BF16).astype(F32)
        ky_ref[f] = jnp.where(part == 2, val - hi, hi).astype(BF16)

        def x_rows(i, _):
            r0 = pl.multiple_of(i * 16, 16)
            row = lax.broadcasted_iota(jnp.int32, (16, 128), 0) + r0
            col = lax.broadcasted_iota(jnp.int32, (16, 128), 1)
            hi, lo = split(fill_tap(row - col + HALF, tx, f == 1))
            wx_ref[f, pl.ds(r0, 16), 0:128] = hi
            wx_ref[f, pl.ds(r0, 16), 128:256] = lo
            r1 = pl.multiple_of(r0 + 128, 16)
            wx_ref[f, pl.ds(r1, 16), 0:128] = hi
            wx_ref[f, pl.ds(r1, 16), 128:256] = jnp.zeros((16, 128), BF16)
            return 0

        lax.fori_loop(0, 8, x_rows, 0)


def z_blur(ext, kz):
    cols = [ext[:, 8 * g : 8 * g + 8, :].reshape(64 * 8, X) for g in range(YC // 8)]
    hi, lo = split(jnp.concatenate(cols, axis=1))
    stack = jnp.concatenate([hi, lo, hi], axis=0)
    return jnp.dot(kz, stack, preferred_element_type=F32)


def y_blur(planes, ky):
    hi, lo = split(jnp.concatenate(planes, axis=1))
    stack = jnp.concatenate([hi, lo, hi], axis=0)
    return jnp.dot(ky, stack, preferred_element_type=F32)


def x_blur(rows, wx):
    hi, lo = split(rows)
    out = jnp.dot(jnp.concatenate([hi, lo], axis=1), wx, preferred_element_type=F32)
    return out[:, :X] + out[:, X:]


def kernel(
    bounds_ref, taps_ref, est_ref, data_ref, out_ref,
    ef, ya, rb, eb, lg, rr, newf, dv, kz, ky, wx,
    lsem, zs, zr, ys, yr, rs_s, rs_r, ag_s, ag_r,
):
    b = lax.axis_index("block")
    v = lax.axis_index("view")
    vx, vy = lax.rem(v, VIEW_X), lax.div(v, VIEW_X)
    bz, by = lax.div(b, BY), lax.rem(b, BY)
    n_bz = lax.axis_size("block") // BY
    has_zlo, has_zhi = bz > 0, bz < n_bz - 1
    has_ylo, has_yhi = by > 0, by < BY - 1

    peers = []
    for dy in range(VIEW_Y):
        for dx in range(VIEW_X):
            if dx or dy:
                to = lax.rem(vy + dy, VIEW_Y) * VIEW_X + lax.rem(vx + dx, VIEW_X)
                frm = lax.rem(vy + VIEW_Y - dy, VIEW_Y) * VIEW_X + lax.rem(vx + VIEW_X - dx, VIEW_X)
                peers.append((to, frm))

    load_est = pltpu.make_async_copy(est_ref.at[0], ef.at[0, pl.ds(PAD, Z)], lsem.at[0])
    load_data = pltpu.make_async_copy(data_ref.at[0, 0], dv, lsem.at[1])
    load_est.start()
    load_data.start()

    bar = pltpu.get_barrier_semaphore()
    total = jnp.int32(VIEWS - 1)
    for cond, dst in ((has_zlo, b - BY), (has_zhi, b + BY), (has_ylo, b - 1), (has_yhi, b + 1)):
        total = total + cond.astype(jnp.int32)

        @pl.when(cond)
        def _():
            pl.semaphore_signal(bar, inc=1, device_id={"block": dst}, device_id_type=MESH)

    for to, _ in peers:
        pl.semaphore_signal(bar, inc=1, device_id={"view": to}, device_id_type=MESH)

    for it in range(ITERS):
        for buf in (ef, eb):
            buf[it, 0] = jnp.zeros((Y, X), F32)
            buf[it, 63] = jnp.zeros((Y, X), F32)

            @pl.when(jnp.logical_not(has_zlo))
            def _():
                buf[it, 1:PAD] = jnp.zeros((HALF, Y, X), F32)

            @pl.when(jnp.logical_not(has_zhi))
            def _():
                buf[it, PAD + Z : PAD + Z + HALF] = jnp.zeros((HALF, Y, X), F32)

        for buf in (ya, rb):

            @pl.when(jnp.logical_not(has_ylo))
            def _():
                buf[it, :, 0:PAD, :] = jnp.zeros((Z, PAD, X), F32)

            @pl.when(jnp.logical_not(has_yhi))
            def _():
                buf[it, :, PAD + Y :, :] = jnp.zeros((Z, PAD, X), F32)

    load_est.wait()
    load_data.wait()
    pl.semaphore_wait(bar, total)

    def z_copies(buf, it, which, j):
        rows = pl.ds(YC * j, YC)
        up = pltpu.make_async_remote_copy(
            src_ref=buf.at[it, pl.ds(PAD + Z - HALF, HALF), rows],
            dst_ref=buf.at[it, pl.ds(1, HALF), rows],
            send_sem=zs.at[it, which, 0, j], recv_sem=zr.at[it, which, 0, j],
            device_id={"block": b + BY}, device_id_type=MESH)
        down = pltpu.make_async_remote_copy(
            src_ref=buf.at[it, pl.ds(PAD, HALF), rows],
            dst_ref=buf.at[it, pl.ds(PAD + Z, HALF), rows],
            send_sem=zs.at[it, which, 1, j], recv_sem=zr.at[it, which, 1, j],
            device_id={"block": b - BY}, device_id_type=MESH)
        return up, down

    def y_copies(buf, it, which, c):
        planes = pl.ds(ZC * c, ZC)
        up = pltpu.make_async_remote_copy(
            src_ref=buf.at[it, planes, pl.ds(Y, PAD)],
            dst_ref=buf.at[it, planes, pl.ds(0, PAD)],
            send_sem=ys.at[it, which, 0, c], recv_sem=yr.at[it, which, 0, c],
            device_id={"block": b + 1}, device_id_type=MESH)
        down = pltpu.make_async_remote_copy(
            src_ref=buf.at[it, planes, pl.ds(PAD, PAD)],
            dst_ref=buf.at[it, planes, pl.ds(PAD + Y, PAD)],
            send_sem=ys.at[it, which, 1, c], recv_sem=yr.at[it, which, 1, c],
            device_id={"block": b - 1}, device_id_type=MESH)
        return up, down

    def start(pair, lo, hi):
        up, down = pair

        @pl.when(hi)
        def _():
            up.start()

        @pl.when(lo)
        def _():
            down.start()

    def wait_recv(pair, lo, hi):
        up, down = pair

        @pl.when(lo)
        def _():
            up.wait_recv()

        @pl.when(hi)
        def _():
            down.wait_recv()

    def wait_send(pair, lo, hi):
        up, down = pair

        @pl.when(hi)
        def _():
            up.wait_send()

        @pl.when(lo)
        def _():
            down.wait_send()

    zsent, ysent, vsent = [], [], []

    def send_z(buf, it, which, j):
        pair = z_copies(buf, it, which, j)
        start(pair, has_zlo, has_zhi)
        zsent.append(pair)

    def send_y(buf, it, which, c):
        pair = y_copies(buf, it, which, c)
        start(pair, has_ylo, has_yhi)
        ysent.append(pair)

    for j in ORDER:
        send_z(ef, 0, 0, j)

    taps = taps_ref[0]
    taps = taps / jnp.sum(taps, axis=1, keepdims=True)
    build_matrices(taps, kz, ky, wx)

    z0, y0 = bz * Z, by * Y
    ypos = lax.broadcasted_iota(jnp.int32, (Y, X), 0) + y0
    own_y = jnp.where((ypos >= bounds_ref[v, 2]) & (ypos < bounds_ref[v, 3]), 1.0, 0.0).astype(F32)

    def own_z(plane):
        zpos = z0 + plane
        return (zpos >= bounds_ref[v, 0]) & (zpos < bounds_ref[v, 1])

    for it in range(ITERS):
        for j in ORDER:
            wait_recv(z_copies(ef, it, 0, j), has_zlo, has_zhi)
            res = z_blur(ef[it, :, YC * j : YC * (j + 1), :], kz[0])
            for g in range(YC // 8):
                r0 = PAD + YC * j + 8 * g
                ya[it, :, r0 : r0 + 8, :] = res[:, X * g : X * (g + 1)].reshape(Z, 8, X)
        for c in range(NZC):
            send_y(ya, it, 0, c)
        for c in range(NZC):
            wait_recv(y_copies(ya, it, 0, c), has_ylo, has_yhi)
            parts = []
            for p in range(ZC * c, ZC * (c + 1), 2):
                res = y_blur([ya[it, p], ya[it, p + 1]], ky[0][:, :240])
                parts += [res[:, :X], res[:, X:]]
            blurred = x_blur(jnp.concatenate(parts, axis=0), wx[0])
            ratio = dv[ZC * c : ZC * (c + 1)].reshape(ZC * Y, X) / blurred
            rb[it, ZC * c : ZC * (c + 1), PAD : PAD + Y, :] = x_blur(ratio, wx[1]).reshape(ZC, Y, X)
            send_y(rb, it, 1, c)
        for c in range(NZC):
            wait_recv(y_copies(rb, it, 1, c), has_ylo, has_yhi)
            for p in range(ZC * c, ZC * (c + 1), 2):
                res = y_blur([rb[it, p], rb[it, p + 1]], ky[1][:, :240])
                eb[it, PAD + p] = res[:, :X]
                eb[it, PAD + p + 1] = res[:, X:]
        for j in ORDER:
            send_z(eb, it, 1, j)
        for j in ORDER:
            wait_recv(z_copies(eb, it, 1, j), has_zlo, has_zhi)
            res = z_blur(eb[it, :, YC * j : YC * (j + 1), :], kz[1])
            for g in range(YC // 8):
                r0 = YC * j + 8 * g
                logs = jnp.log(res[:, X * g : X * (g + 1)].reshape(Z, 8, X))
                for p in range(Z):
                    keep = jnp.where(own_z(p), own_y[r0 : r0 + 8], 0.0)
                    lg[it, p, r0 : r0 + 8, :] = keep * logs[p]
            rows = pl.ds(YC * j, YC)
            for i, (to, frm) in enumerate(peers):
                cp = pltpu.make_async_remote_copy(
                    src_ref=lg.at[it, pl.ds(to * PIECE, PIECE), rows],
                    dst_ref=rr.at[it, i, :, rows],
                    send_sem=rs_s.at[it, i, j], recv_sem=rs_r.at[it, i, j],
                    device_id={"view": to}, device_id_type=MESH)
                cp.start()
                vsent.append(cp)
        mine = v * PIECE
        for j in ORDER:
            rows = pl.ds(YC * j, YC)
            acc = lg[it, pl.ds(mine, PIECE), YC * j : YC * (j + 1), :]
            for i in range(VIEWS - 1):
                pltpu.make_async_remote_copy(
                    src_ref=lg.at[it, pl.ds(0, PIECE), rows], dst_ref=rr.at[it, i, :, rows],
                    send_sem=rs_s.at[it, i, j], recv_sem=rs_r.at[it, i, j],
                    device_id={"view": peers[i][0]}, device_id_type=MESH).wait_recv()
                acc = acc + rr[it, i, :, YC * j : YC * (j + 1), :]
            yj = ypos[YC * j : YC * (j + 1)]
            ins = [
                jnp.where((yj >= bounds_ref[w, 2]) & (yj < bounds_ref[w, 3]), 1.0, 0.0).astype(F32)
                for w in range(VIEWS)
            ]
            for p in range(PIECE):
                zpos = z0 + mine + p
                count = jnp.zeros((YC, X), F32)
                for w in range(VIEWS):
                    inz = (zpos >= bounds_ref[w, 0]) & (zpos < bounds_ref[w, 1])
                    count = count + jnp.where(inz, ins[w], 0.0)
                old = ef[it, PAD + mine + p, YC * j : YC * (j + 1), :]
                new = old * jnp.exp(acc[p] / count)
                newf[it, p, YC * j : YC * (j + 1), :] = new
                if it < ITERS - 1:
                    ef[it + 1, PAD + mine + p, YC * j : YC * (j + 1), :] = new
            if it < ITERS - 1:
                target = ef.at[it + 1, pl.ds(PAD + mine, PIECE), rows]
            else:
                target = out_ref.at[0, pl.ds(mine, PIECE), rows]
                cp = pltpu.make_async_copy(newf.at[it, :, rows], target, lsem.at[2 + j])
                cp.start()
                vsent.append(cp)
            for i, (to, frm) in enumerate(peers):
                cp = pltpu.make_async_remote_copy(
                    src_ref=newf.at[it, :, rows], dst_ref=target,
                    send_sem=ag_s.at[it, i, j], recv_sem=ag_r.at[it, i, j],
                    device_id={"view": to}, device_id_type=MESH)
                cp.start()
                vsent.append(cp)
        for j in ORDER:
            rows = pl.ds(YC * j, YC)
            for i, (to, frm) in enumerate(peers):
                if it < ITERS - 1:
                    target = ef.at[it + 1, pl.ds(PAD + frm * PIECE, PIECE), rows]
                else:
                    target = out_ref.at[0, pl.ds(frm * PIECE, PIECE), rows]
                pltpu.make_async_remote_copy(
                    src_ref=newf.at[it, :, rows], dst_ref=target,
                    send_sem=ag_s.at[it, i, j], recv_sem=ag_r.at[it, i, j],
                    device_id={"view": to}, device_id_type=MESH).wait_recv()
            if it < ITERS - 1:
                send_z(ef, it + 1, 0, j)

    for pair in zsent:
        wait_send(pair, has_zlo, has_zhi)
    for pair in ysent:
        wait_send(pair, has_ylo, has_yhi)
    for cp in vsent:
        if cp.is_remote:
            cp.wait_send()
        else:
            cp.wait()


def body(estimate, views_data, psf_taps, view_bounds):
    dma = pltpu.SemaphoreType.DMA
    return pl.pallas_call(
        kernel,
        out_shape=jax.ShapeDtypeStruct(estimate.shape, F32),
        in_specs=[
            pl.BlockSpec(memory_space=pltpu.SMEM),
            pl.BlockSpec(memory_space=pltpu.VMEM),
            pl.BlockSpec(memory_space=pl.ANY),
            pl.BlockSpec(memory_space=pl.ANY),
        ],
        out_specs=pl.BlockSpec(memory_space=pl.ANY),
        scratch_shapes=[
            pltpu.VMEM((ITERS, 64, Y, X), F32),
            pltpu.VMEM((ITERS, Z, 80, X), F32),
            pltpu.VMEM((ITERS, Z, 80, X), F32),
            pltpu.VMEM((ITERS, 64, Y, X), F32),
            pltpu.VMEM((ITERS, Z, Y, X), F32),
            pltpu.VMEM((ITERS, VIEWS - 1, PIECE, Y, X), F32),
            pltpu.VMEM((ITERS, PIECE, Y, X), F32),
            pltpu.VMEM((Z, Y, X), F32),
            pltpu.VMEM((2, 256, 1536), BF16),
            pltpu.VMEM((2, Y, 256), BF16),
            pltpu.VMEM((2, 256, 256), BF16),
            dma((2 + NJ,)),
            dma((ITERS, 2, 2, NJ)),
            dma((ITERS, 2, 2, NJ)),
            dma((ITERS, 2, 2, NZC)),
            dma((ITERS, 2, 2, NZC)),
            dma((ITERS, VIEWS - 1, NJ)),
            dma((ITERS, VIEWS - 1, NJ)),
            dma((ITERS, VIEWS - 1, NJ)),
            dma((ITERS, VIEWS - 1, NJ)),
        ],
        compiler_params=pltpu.CompilerParams(
            collective_id=0, has_side_effects=True, vmem_limit_bytes=48 << 20
        ),
        name="deconvolve",
    )(view_bounds, psf_taps, estimate, views_data)


def solution(mesh):
    return jax.shard_map(
        body,
        mesh=mesh,
        in_specs=(
            P("block", None, None, None),
            P("view", "block", None, None, None),
            P("view", None, None),
            P(),
        ),
        out_specs=P("block", None, None, None),
        check_vma=False,
    )
```

time: 632 us -> 141 us (0.22); the launches traced: 624 us -> 141 us
  waiting for transfers between devices: 273 us -> 0 us
  other arithmetic: 186 us -> 0 us
  Pallas kernels: 0 us -> 137 us
  matrix products: 82 us -> 0 us
  starting transfers between devices: 61.2 us -> 0 us
  between operations: 13.9 us -> 0.01 us
    psum x2 -> x0, waiting for transfers between devices: 204 us -> none  [view_sum(): return lax.psum(logs, 'view')]
    pallas_call x0 -> x1, Pallas kernels: none -> 137 us  [body(): pl.pallas_call(kernel, out_shape=jax.ShapeDtypeStruct(estimate.shape, F32...]
    add x6 -> x0, other arithmetic: 86.7 us -> none  [the longest x4 86.7 us: tap_sum(): total + taps[tap] * lax.slice_in_dim(extended, tap, tap + length, axis=axis)]
    dot_general x4 -> x0, matrix products: 82 us -> none  [along_x(): jnp.dot(flat, matrix, precision=lax.Precision.HIGHEST, preferred_element_...]
    ppermute x16 -> x0, waiting for transfers between devices: 69.1 us -> none  [from_behind(): lax.ppermute(value, axis, [(source, source + steps) for source in range(f...]
    ppermute x16 -> x0, starting transfers between devices: 61.2 us -> none  [from_behind(): lax.ppermute(value, axis, [(source, source + steps) for source in range(f...]
    mul x4 -> x0, other arithmetic: 49.5 us -> none  [the longest x3 48.1 us: body(): logs = own_masks[0] * jnp.log(correction)]
    div x3 -> x0, other arithmetic: 46.7 us -> none  [the longest x2 46 us: body(): ratio = views_data[0, 0] / blurred]
  transfers between devices with their start and end apart: 18 -> 0, of which waited for: 13 -> 0; matrix products, arithmetic and copies ran while one was open for 1% -> 0% of each run, Pallas kernels for 0% -> 0%
where the time goes in v1:
time: 141 us
  Pallas kernels  137 us (97%)
  local copies, waits for them, and re-layouts  3.93 us (3%)
    pallas_call x1, Pallas kernels, body(): pl.pallas_call(kernel, out_shape=jax.ShapeDtypeStruct(estimate.shape, F32...  137 us
    unnamed x9, local copies, waits for them, and re-layouts  3.93 us

profile of v1, /device:TPU:1, one launch (start us, length us, event | category | flops | bytes accessed | tf_op | source)
XLA Modules:
  0.0 141.0 jit_solution(7956693198314679374)
XLA Ops:
  0.0 0.0 copy-start.2
  0.0 0.7 copy.6.taps_ref
  0.7 0.0 copy-done.2
  0.7 0.1 copy.5.bounds_ref
  0.8 0.0 copy-start
  0.8 1.1 copy-done
  1.9 0.0 copy-start.1
  1.9 1.1 copy-done.1
  3.0 137.0 %deconvolve.1 = f32[1,32,48,128]{3,2,1,0:T(8,128)S(1)} custom-call(s32[8,4]{1,0:T(8,128)S(1)} %copy.5.bounds_ref, f32[1,3,31]{2,1,0:T(4,128)S(1)} %copy.6.taps_ref, f32[1,32,48,128]{3,2,1,0:T(8,128)S(1)} %copy-done, f32[1,1,32,48,128]{4,3,2,1,0:T(8,128)S(1)} %copy-done.1), custom_call_target="tpu_custom_call" | custom-call | tf_op jit(solution)/shard_map/deconvolve/pallas_call | solution.py:369
  140.1 0.9 copy.8
Async XLA Ops:
  0.0 0.7 copy-start.2
  0.8 1.1 copy-start
  1.9 1.1 copy-start.1

commit v2 on v1

v2 whole, which is shorter than its diff:
```python
import functools

import jax
import jax.numpy as jnp
from jax import lax
from jax.experimental import pallas as pl
from jax.experimental.pallas import tpu as pltpu
from jax.sharding import PartitionSpec as P

MESH = pl.DeviceIdType.MESH
F32 = jnp.float32
BF16 = jnp.bfloat16

BY = 4
ITERS = 2
Z, Y, X = 32, 48, 128
TAPS = 31
HALF = 15
PAD = 16
VIEW_X, VIEW_Y = 4, 2
VIEWS = VIEW_X * VIEW_Y
PIECE = Z // VIEWS
YC = 8
NJ = Y // YC
ORDER = (2, 3, 0, 1, 4, 5)
FIRST_YC = 16
FIRST_NJ = Y // FIRST_YC
FIRST = (0, 2, 1)
DIRECT = HALF - VIEWS
ZC = 8
NZC = Z // ZC


def split(x):
    hi = x.astype(BF16)
    lo = (x - hi.astype(F32)).astype(BF16)
    return hi, lo


def fill_tap(offset, taps, flip):
    acc = jnp.zeros(offset.shape, F32)
    for k in range(TAPS):
        at = TAPS - 1 - k if flip else k
        acc = jnp.where(offset == k, taps[:, at : at + 1], acc)
    return acc


def build_z(taps, kz_ref, f):
    def z_rows(i, _):
        r0 = pl.multiple_of(i * 16, 16)
        row = lax.broadcasted_iota(jnp.int32, (16, 512), 0) + r0
        col = lax.broadcasted_iota(jnp.int32, (16, 512), 1)
        k = jnp.where((col & 7) == (row & 7), (col >> 3) - 1 - (row >> 3), -1)
        hi, lo = split(fill_tap(k, taps[0], f == 1))
        kz_ref[f, pl.ds(r0, 16), 0:512] = hi
        kz_ref[f, pl.ds(r0, 16), 512:1024] = hi
        kz_ref[f, pl.ds(r0, 16), 1024:1536] = lo
        return 0

    lax.fori_loop(0, 16, z_rows, 0)


def build_xy(taps, ko_ref, kr_ref, wx_ref, f):
    row = lax.broadcasted_iota(jnp.int32, (Y, 256), 0)
    col = lax.broadcasted_iota(jnp.int32, (Y, 256), 1)
    part = jnp.where(col >= 96, 2, jnp.where(col >= 48, 1, 0))
    k = jnp.where(col < 144, col - 48 * part - row + HALF, -1)
    val = fill_tap(k, taps[1], f == 1)
    hi = val.astype(BF16).astype(F32)
    ko_ref[f] = jnp.where(part == 2, val - hi, hi).astype(BF16)

    row = lax.broadcasted_iota(jnp.int32, (2 * PAD, 128), 0)
    col = lax.broadcasted_iota(jnp.int32, (2 * PAD, 128), 1)
    part = jnp.where(col >= 64, 2, jnp.where(col >= 32, 1, 0))
    at = col - 32 * part
    source = jnp.where(at < PAD, at - PAD, at + Y - PAD)
    target = jnp.where(row < PAD, row, row + Y - 2 * PAD)
    k = jnp.where(col < 96, source - target + HALF, -1)
    val = fill_tap(k, taps[1], f == 1)
    hi = val.astype(BF16).astype(F32)
    kr_ref[f] = jnp.where(part == 2, val - hi, hi).astype(BF16)

    def x_rows(i, _):
        r0 = pl.multiple_of(i * 16, 16)
        row = lax.broadcasted_iota(jnp.int32, (16, 128), 0) + r0
        col = lax.broadcasted_iota(jnp.int32, (16, 128), 1)
        hi, lo = split(fill_tap(row - col + HALF, taps[2], f == 1))
        wx_ref[f, pl.ds(r0, 16), 0:128] = hi
        wx_ref[f, pl.ds(r0, 16), 128:256] = lo
        r1 = pl.multiple_of(r0 + 128, 16)
        wx_ref[f, pl.ds(r1, 16), 0:128] = hi
        wx_ref[f, pl.ds(r1, 16), 128:256] = jnp.zeros((16, 128), BF16)
        return 0

    lax.fori_loop(0, 8, x_rows, 0)


def z_blur(ext, kz):
    cols = [ext[:, 8 * g : 8 * g + 8, :].reshape(64 * 8, X) for g in range(ext.shape[1] // 8)]
    hi, lo = split(jnp.concatenate(cols, axis=1))
    stack = jnp.concatenate([hi, lo, hi], axis=0)
    return jnp.dot(kz, stack, preferred_element_type=F32)


def y_blur(planes, ky):
    hi, lo = split(jnp.concatenate(planes, axis=1))
    stack = jnp.concatenate([hi, lo, hi], axis=0)
    return jnp.dot(ky, stack, preferred_element_type=F32)


def x_blur(rows, wx):
    hi, lo = split(rows)
    out = jnp.dot(jnp.concatenate([hi, lo], axis=1), wx, preferred_element_type=F32)
    return out[:, :X] + out[:, X:]


def kernel(
    bounds_ref, taps_ref, est_ref, data_ref, out_ref,
    ef, ya, rb, eb, lg, rr, newf, dv, pa, taps_v, kz, ko, kr, wx,
    lsem, zs, zr, hs, hr, fs, fr, ys, yr, rs_s, rs_r, ag_s, ag_r,
):
    b = lax.axis_index("block")
    v = lax.axis_index("view")
    vx, vy = lax.rem(v, VIEW_X), lax.div(v, VIEW_X)
    bz, by = lax.div(b, BY), lax.rem(b, BY)
    n_bz = lax.axis_size("block") // BY
    has_zlo, has_zhi = bz > 0, bz < n_bz - 1
    has_ylo, has_yhi = by > 0, by < BY - 1

    peers = []
    for dy in range(VIEW_Y):
        for dx in range(VIEW_X):
            if dx or dy:
                to = lax.rem(vy + dy, VIEW_Y) * VIEW_X + lax.rem(vx + dx, VIEW_X)
                frm = lax.rem(vy + VIEW_Y - dy, VIEW_Y) * VIEW_X + lax.rem(vx + VIEW_X - dx, VIEW_X)
                peers.append((to, frm))

    load_est = pltpu.make_async_copy(est_ref.at[0], ef.at[0, pl.ds(PAD, Z)], lsem.at[0])
    load_data = pltpu.make_async_copy(data_ref.at[0, 0], dv, lsem.at[1])
    load_taps = pltpu.make_async_copy(taps_ref, taps_v, lsem.at[2])
    load_est.start()
    load_data.start()
    load_taps.start()

    bar = pltpu.get_barrier_semaphore()
    total = jnp.int32(VIEWS - 1)
    for cond, dst in ((has_zlo, b - BY), (has_zhi, b + BY), (has_ylo, b - 1), (has_yhi, b + 1)):
        total = total + cond.astype(jnp.int32)

        @pl.when(cond)
        def _():
            pl.semaphore_signal(bar, inc=1, device_id={"block": dst}, device_id_type=MESH)

    for to, _ in peers:
        pl.semaphore_signal(bar, inc=1, device_id={"view": to}, device_id_type=MESH)

    for it in range(ITERS):
        for buf in (ef, eb):
            buf[it, 0] = jnp.zeros((Y, X), F32)
            buf[it, 63] = jnp.zeros((Y, X), F32)

        @pl.when(jnp.logical_not(has_zlo))
        def _():
            eb[it, 1:PAD] = jnp.zeros((HALF, Y, X), F32)

        @pl.when(jnp.logical_not(has_zhi))
        def _():
            eb[it, PAD + Z : PAD + Z + HALF] = jnp.zeros((HALF, Y, X), F32)

        low = pl.ds(1, HALF) if it else pl.ds(1 + VIEWS, DIRECT)
        high = pl.ds(PAD + Z, HALF if it else DIRECT)

        @pl.when(jnp.logical_not(has_zlo))
        def _():
            if it == 0:
                ef[it, 1 + v] = jnp.zeros((Y, X), F32)
            ef[it, low] = jnp.zeros((low.size, Y, X), F32)

        @pl.when(jnp.logical_not(has_zhi))
        def _():
            if it == 0:
                ef[it, PAD + Z + DIRECT + v] = jnp.zeros((Y, X), F32)
            ef[it, high] = jnp.zeros((high.size, Y, X), F32)

        for buf in (ya, rb):

            @pl.when(jnp.logical_not(has_ylo))
            def _():
                buf[it, :, 0:PAD, :] = jnp.zeros((Z, PAD, X), F32)

            @pl.when(jnp.logical_not(has_yhi))
            def _():
                buf[it, :, PAD + Y :, :] = jnp.zeros((Z, PAD, X), F32)

    load_est.wait()
    pl.semaphore_wait(bar, total)

    def pair_of(buf, it, up, down, count, rows, sems, recvs, key, step):
        one = pltpu.make_async_remote_copy(
            src_ref=buf.at[it, pl.ds(up[0], count), rows], dst_ref=buf.at[it, pl.ds(up[1], count), rows],
            send_sem=sems.at[(it, 0) + key], recv_sem=recvs.at[(it, 0) + key],
            device_id={"block": b + step}, device_id_type=MESH)
        two = pltpu.make_async_remote_copy(
            src_ref=buf.at[it, pl.ds(down[0], count), rows], dst_ref=buf.at[it, pl.ds(down[1], count), rows],
            send_sem=sems.at[(it, 1) + key], recv_sem=recvs.at[(it, 1) + key],
            device_id={"block": b - step}, device_id_type=MESH)
        return one, two

    def ratio_rims(it, j):
        rows = pl.ds(YC * j, YC)
        return pair_of(eb, it, (PAD + Z - HALF, 1), (PAD, PAD + Z), HALF, rows, zs, zr, (1, j), BY)

    def estimate_rims(it, j):
        rows = pl.ds(YC * j, YC)
        return pair_of(ef, it, (PAD + Z - HALF, 1), (PAD, PAD + Z), HALF, rows, zs, zr, (0, j), BY)

    def direct_rims(j):
        rows = pl.ds(FIRST_YC * j, FIRST_YC)
        return pair_of(ef, 0, (PAD + Z - DIRECT, 1 + VIEWS), (PAD, PAD + Z), DIRECT, rows, zs, zr, (0, j), BY)

    def shared_rims(j):
        rows = pl.ds(FIRST_YC * j, FIRST_YC)
        return pair_of(ef, 0, (PAD + 17 + v, 1 + v), (PAD + DIRECT + v, PAD + Z + DIRECT + v), 1, rows, hs, hr, (j,), BY)

    def forwards(j, w):
        rows = pl.ds(FIRST_YC * j, FIRST_YC)
        out = []
        for i, (to, frm) in enumerate(peers):
            for h, first in enumerate((1, PAD + Z + DIRECT)):
                plane = pl.ds(first + (v if w else frm), 1)
                out.append(pltpu.make_async_remote_copy(
                    src_ref=ef.at[0, plane, rows], dst_ref=ef.at[0, plane, rows],
                    send_sem=fs.at[h, i, j], recv_sem=fr.at[h, i, j],
                    device_id={"view": to}, device_id_type=MESH))
        return out

    def y_pair(buf, it, which, planes, n, c, half):
        up = pltpu.make_async_remote_copy(
            src_ref=buf.at[it, planes, pl.ds(Y + half, n)], dst_ref=buf.at[it, planes, pl.ds(half, n)],
            send_sem=ys.at[it, which, 0, c], recv_sem=yr.at[it, which, 0, c],
            device_id={"block": b + 1}, device_id_type=MESH)
        down = pltpu.make_async_remote_copy(
            src_ref=buf.at[it, planes, pl.ds(PAD + half, n)], dst_ref=buf.at[it, planes, pl.ds(PAD + Y + half, n)],
            send_sem=ys.at[it, which, 1, c], recv_sem=yr.at[it, which, 1, c],
            device_id={"block": b - 1}, device_id_type=MESH)
        return up, down

    def blurred_rims(it, h):
        return y_pair(ya, it, 0, pl.ds(0, Z), 8, h, 8 * h)

    def ratio_y_rims(it, c):
        return y_pair(rb, it, 1, pl.ds(ZC * c, ZC), PAD, c, 0)

    def start(pair, lo, hi):
        up, down = pair

        @pl.when(hi)
        def _():
            up.start()

        @pl.when(lo)
        def _():
            down.start()

    def wait_recv(pair, lo, hi):
        up, down = pair

        @pl.when(lo)
        def _():
            up.wait_recv()

        @pl.when(hi)
        def _():
            down.wait_recv()

    def wait_send(pair, lo, hi):
        up, down = pair

        @pl.when(hi)
        def _():
            up.wait_send()

        @pl.when(lo)
        def _():
            down.wait_send()

    zsent, ysent, vsent = [], [], []

    def send_z(pair):
        start(pair, has_zlo, has_zhi)
        zsent.append(pair)

    def send_y(up, down):
        if up is not None:

            @pl.when(has_yhi)
            def _():
                up.start()

            ysent.append((has_yhi, up))
        if down is not None:

            @pl.when(has_ylo)
            def _():
                down.start()

            ysent.append((has_ylo, down))

    def start_up(pair):
        @pl.when(has_zhi)
        def _():
            pair[0].start()

    def start_down(pair):
        @pl.when(has_zlo)
        def _():
            pair[1].start()

    for j in FIRST:
        send_z(shared_rims(j))
    for j in FIRST:
        send_z(direct_rims(j))

    load_taps.wait()
    taps = taps_v[...]
    taps = taps / jnp.sum(taps, axis=2, keepdims=True)
    build_z(taps, kz, 0)

    z0, y0 = bz * Z, by * Y
    ypos = lax.broadcasted_iota(jnp.int32, (Y, X), 0) + y0
    own_y = jnp.where((ypos >= bounds_ref[2, v]) & (ypos < bounds_ref[3, v]), 1.0, 0.0).astype(F32)

    def own_z(plane):
        zpos = z0 + plane
        return (zpos >= bounds_ref[0, v]) & (zpos < bounds_ref[1, v])

    def blur_rows(it, r0, rows):
        res = z_blur(ef[it, :, r0 : r0 + rows, :], kz[0])
        for r in range(r0, r0 + rows, 8):
            at = X * ((r - r0) // 8)
            ya[it, :, PAD + r : PAD + r + 8, :] = res[:, at : at + X].reshape(Z, 8, X)
            if r < PAD:
                send_y(None, blurred_rims(it, r // 8)[1])
            if r >= Y - PAD:
                send_y(blurred_rims(it, (r - Y + PAD) // 8)[0], None)

    for j in FIRST:
        wait_recv(shared_rims(j), has_zlo, has_zhi)
        for cp in forwards(j, True):
            cp.start()
            vsent.append(cp)
    build_xy(taps, ko, kr, wx, 0)
    build_xy(taps, ko, kr, wx, 1)
    build_z(taps, kz, 1)
    load_data.wait()
    for j in FIRST:
        wait_recv(direct_rims(j), has_zlo, has_zhi)
        for cp in forwards(j, False):
            cp.wait_recv()
        blur_rows(0, FIRST_YC * j, FIRST_YC)

    for it in range(ITERS):
        own = slice(PAD, PAD + Y)
        for p in range(0, Z, 2):
            res = y_blur([ya[it, p, own], ya[it, p + 1, own]], ko[0][:, :144])
            pa[p] = res[:, :X]
            pa[p + 1] = res[:, X:]
        for h in range(2):
            wait_recv(blurred_rims(it, h), has_ylo, has_yhi)

        def rims(buf, p):
            return jnp.concatenate([buf[it, p, 0:PAD], buf[it, p, PAD + Y :]], axis=0)

        for c in range(NZC):
            span = range(ZC * c, ZC * (c + 1), 2)
            parts = []
            for p in span:
                res = y_blur([rims(ya, p), rims(ya, p + 1)], kr[0][:, :96])
                for h in range(2):
                    edge = res[:, X * h : X * (h + 1)]
                    parts += [pa[p + h, 0:PAD] + edge[:PAD], pa[p + h, PAD : 2 * PAD], pa[p + h, 2 * PAD :] + edge[PAD:]]
            blurred = x_blur(jnp.concatenate(parts, axis=0), wx[0])
            ratio = dv[ZC * c : ZC * (c + 1)].reshape(ZC * Y, X) / blurred
            rb[it, ZC * c : ZC * (c + 1), own, :] = x_blur(ratio, wx[1]).reshape(ZC, Y, X)
            send_y(*ratio_y_rims(it, c))
            for p in span:
                res = y_blur([rb[it, p, own], rb[it, p + 1, own]], ko[1][:, :144])
                eb[it, PAD + p] = res[:, :X]
                eb[it, PAD + p + 1] = res[:, X:]
            if c == NZC // 2 - 1:
                for j in ORDER[:2]:
                    pair = ratio_rims(it, j)
                    zsent.append(pair)
                    start_down(pair)
        for j in ORDER[:2]:
            start_up(ratio_rims(it, j))
        for c in range(NZC):
            wait_recv(ratio_y_rims(it, c), has_ylo, has_yhi)
            for p in range(ZC * c, ZC * (c + 1), 2):
                res = y_blur([rims(rb, p), rims(rb, p + 1)], kr[1][:, :96])
                for h in range(2):
                    edge = res[:, X * h : X * (h + 1)]
                    eb[it, PAD + p + h, 0:PAD] += edge[:PAD]
                    eb[it, PAD + p + h, 2 * PAD :] += edge[PAD:]
            if c == NZC // 2 - 1:
                for j in ORDER[2:]:
                    pair = ratio_rims(it, j)
                    zsent.append(pair)
                    start_down(pair)
        for j in ORDER[2:]:
            start_up(ratio_rims(it, j))

        mine = v * PIECE

        def log_step(j):
            wait_recv(ratio_rims(it, j), has_zlo, has_zhi)
            res = z_blur(eb[it, :, YC * j : YC * (j + 1), :], kz[1])
            for g in range(YC // 8):
                r0 = YC * j + 8 * g
                logs = jnp.log(res[:, X * g : X * (g + 1)].reshape(Z, 8, X))
                for p in range(Z):
                    keep = jnp.where(own_z(p), own_y[r0 : r0 + 8], 0.0)
                    lg[it, p, r0 : r0 + 8, :] = keep * logs[p]
            rows = pl.ds(YC * j, YC)
            for i, (to, frm) in enumerate(peers):
                cp = pltpu.make_async_remote_copy(
                    src_ref=lg.at[it, pl.ds(to * PIECE, PIECE), rows],
                    dst_ref=rr.at[it, i, :, rows],
                    send_sem=rs_s.at[it, i, j], recv_sem=rs_r.at[it, i, j],
                    device_id={"view": to}, device_id_type=MESH)
                cp.start()
                vsent.append(cp)

        def sum_step(j):
            rows = pl.ds(YC * j, YC)
            acc = lg[it, pl.ds(mine, PIECE), YC * j : YC * (j + 1), :]
            for i in range(VIEWS - 1):
                pltpu.make_async_remote_copy(
                    src_ref=lg.at[it, pl.ds(0, PIECE), rows], dst_ref=rr.at[it, i, :, rows],
                    send_sem=rs_s.at[it, i, j], recv_sem=rs_r.at[it, i, j],
                    device_id={"view": peers[i][0]}, device_id_type=MESH).wait_recv()
                acc = acc + rr[it, i, :, YC * j : YC * (j + 1), :]
            yj = ypos[YC * j : YC * (j + 1)]
            ins = [
                jnp.where((yj >= bounds_ref[2, w]) & (yj < bounds_ref[3, w]), 1.0, 0.0).astype(F32)
                for w in range(VIEWS)
            ]
            for p in range(PIECE):
                zpos = z0 + mine + p
                count = jnp.zeros((YC, X), F32)
                for w in range(VIEWS):
                    inz = (zpos >= bounds_ref[0, w]) & (zpos < bounds_ref[1, w])
                    count = count + jnp.where(inz, ins[w], 0.0)
                old = ef[it, PAD + mine + p, YC * j : YC * (j + 1), :]
                new = old * jnp.exp(acc[p] / count)
                newf[it, p, YC * j : YC * (j + 1), :] = new
                if it < ITERS - 1:
                    ef[it + 1, PAD + mine + p, YC * j : YC * (j + 1), :] = new
            if it < ITERS - 1:
                target = ef.at[it + 1, pl.ds(PAD + mine, PIECE), rows]
            else:
                target = out_ref.at[0, pl.ds(mine, PIECE), rows]
                cp = pltpu.make_async_copy(newf.at[it, :, rows], target, lsem.at[3 + j])
                cp.start()
                vsent.append(cp)
            for i, (to, frm) in enumerate(peers):
                cp = pltpu.make_async_remote_copy(
                    src_ref=newf.at[it, :, rows], dst_ref=target,
                    send_sem=ag_s.at[it, i, j], recv_sem=ag_r.at[it, i, j],
                    device_id={"view": to}, device_id_type=MESH)
                cp.start()
                vsent.append(cp)

        def gather_step(j):
            rows = pl.ds(YC * j, YC)
            for i, (to, frm) in enumerate(peers):
                if it < ITERS - 1:
                    target = ef.at[it + 1, pl.ds(PAD + frm * PIECE, PIECE), rows]
                else:
                    target = out_ref.at[0, pl.ds(frm * PIECE, PIECE), rows]
                pltpu.make_async_remote_copy(
                    src_ref=newf.at[it, :, rows], dst_ref=target,
                    send_sem=ag_s.at[it, i, j], recv_sem=ag_r.at[it, i, j],
                    device_id={"view": to}, device_id_type=MESH).wait_recv()
            if it < ITERS - 1:
                send_z(estimate_rims(it + 1, j))

        for n in range(NJ + 6):
            if n < NJ:
                log_step(ORDER[n])
            if 0 <= n - 2 < NJ:
                sum_step(ORDER[n - 2])
            if 0 <= n - 4 < NJ:
                gather_step(ORDER[n - 4])
            if 0 <= n - 6 < NJ and it < ITERS - 1:
                j = ORDER[n - 6]
                wait_recv(estimate_rims(it + 1, j), has_zlo, has_zhi)
                blur_rows(it + 1, YC * j, YC)

    for pair in zsent:
        wait_send(pair, has_zlo, has_zhi)
    for cond, cp in ysent:

        @pl.when(cond)
        def _():
            cp.wait_send()

    for cp in vsent:
        if cp.is_remote:
            cp.wait_send()
        else:
            cp.wait()


def body(estimate, views_data, psf_taps, view_bounds):
    dma = pltpu.SemaphoreType.DMA
    return pl.pallas_call(
        kernel,
        out_shape=jax.ShapeDtypeStruct(estimate.shape, F32),
        in_specs=[
            pl.BlockSpec(memory_space=pltpu.SMEM),
            pl.BlockSpec(memory_space=pltpu.HBM),
            pl.BlockSpec(memory_space=pltpu.HBM),
            pl.BlockSpec(memory_space=pltpu.HBM),
        ],
        out_specs=pl.BlockSpec(memory_space=pl.ANY),
        scratch_shapes=[
            pltpu.VMEM((ITERS, 64, Y, X), F32),
            pltpu.VMEM((ITERS, Z, 80, X), F32),
            pltpu.VMEM((ITERS, Z, 80, X), F32),
            pltpu.VMEM((ITERS, 64, Y, X), F32),
            pltpu.VMEM((ITERS, Z, Y, X), F32),
            pltpu.VMEM((ITERS, VIEWS - 1, PIECE, Y, X), F32),
            pltpu.VMEM((ITERS, PIECE, Y, X), F32),
            pltpu.VMEM((Z, Y, X), F32),
            pltpu.VMEM((Z, Y, X), F32),
            pltpu.VMEM((3, 1, TAPS), F32),
            pltpu.VMEM((2, 256, 1536), BF16),
            pltpu.VMEM((2, Y, 256), BF16),
            pltpu.VMEM((2, 2 * PAD, 128), BF16),
            pltpu.VMEM((2, 256, 256), BF16),
            dma((3 + NJ,)),
            dma((ITERS, 2, 2, NJ)),
            dma((ITERS, 2, 2, NJ)),
            dma((1, 2, FIRST_NJ)),
            dma((1, 2, FIRST_NJ)),
            dma((2, VIEWS - 1, FIRST_NJ)),
            dma((2, VIEWS - 1, FIRST_NJ)),
            dma((ITERS, 2, 2, NZC)),
            dma((ITERS, 2, 2, NZC)),
            dma((ITERS, VIEWS - 1, NJ)),
            dma((ITERS, VIEWS - 1, NJ)),
            dma((ITERS, VIEWS - 1, NJ)),
            dma((ITERS, VIEWS - 1, NJ)),
        ],
        compiler_params=pltpu.CompilerParams(
            collective_id=0, has_side_effects=True, vmem_limit_bytes=64000000
        ),
        name="deconvolve",
    )(view_bounds.T, psf_taps.transpose(1, 0, 2), estimate, views_data)


def solution(mesh):
    return jax.shard_map(
        body,
        mesh=mesh,
        in_specs=(
            P("block", None, None, None),
            P("view", "block", None, None, None),
            P("view", None, None),
            P(),
        ),
        out_specs=P("block", None, None, None),
        check_vma=False,
    )
```

time: 141 us -> 127 us (0.901)
  the two profiles are of different devices: /device:TPU:1 before, /device:TPU:96 now
where the time goes in v2:
time: 127 us
  Pallas kernels  125 us (98%)
  local copies, waits for them, and re-layouts  2.06 us (2%)
    pallas_call x1, Pallas kernels, body(): pl.pallas_call(kernel, out_shape=jax.ShapeDtypeStruct(estimate.shape, F32...  125 us

profile of v2, /device:TPU:96, one launch (start us, length us, event | category | flops | bytes accessed | tf_op | source)
XLA Modules:
  0.0 127.3 jit_solution(645361715920048135)
XLA Ops:
  0.0 125.2 %deconvolve.1 = f32[1,32,48,128]{3,2,1,0:T(8,128)} custom-call(s32[4,8]{1,0:T(4,128)} %bitcast.2, f32[3,1,31]{2,1,0:T(1,128)} %bitcast.3, f32[1,32,48,128]{3,2,1,0:T(8,128)} %est_ref.1, f32[1,1,32,48,128]{4,3,2,1,0:T(8,128)} %data_ref.1), custom_call_target="tpu_custom_call" | custom-call | tf_op jit(solution)/shard_map/deconvolve/pallas_call | solution.py:517
  125.2 2.1 %copy.6 = f32[1,32,48,128]{3,2,1,0:T(8,128)} copy(f32[1,32,48,128]{3,2,1,0:T(8,128)} %deconvolve.1) | data formatting | bytes 1572864

commit v3 on v2

--- a/solution.py
+++ b/solution.py
@@ -20,15 +20,15 @@
 VIEW_X, VIEW_Y = 4, 2
 VIEWS = VIEW_X * VIEW_Y
 PIECE = Z // VIEWS
-YC = 8
-NJ = Y // YC
-ORDER = (2, 3, 0, 1, 4, 5)
+CHUNKS = ((16, 16), (0, 16), (32, 8), (40, 8))
+NJ = len(CHUNKS)
 FIRST_YC = 16
 FIRST_NJ = Y // FIRST_YC
 FIRST = (0, 2, 1)
-DIRECT = HALF - VIEWS
+S1, S2, S3 = 3, 5, 7
 ZC = 8
 NZC = Z // ZC
+ZORDER = (0, 3, 1, 2)
 
 
 def split(x):
@@ -45,12 +45,25 @@
     return acc
 
 
+def own_plane(slot):
+    return (slot >> 2) + VIEWS * (slot & 3)
+
+
+def estimate_plane(slot):
+    z = own_plane(slot & (Z - 1))
+    return jnp.where(slot < Z, z, jnp.where((slot & 3) < 2, z + Z, z - Z))
+
+
 def build_z(taps, kz_ref, f):
     def z_rows(i, _):
         r0 = pl.multiple_of(i * 16, 16)
         row = lax.broadcasted_iota(jnp.int32, (16, 512), 0) + r0
         col = lax.broadcasted_iota(jnp.int32, (16, 512), 1)
-        k = jnp.where((col & 7) == (row & 7), (col >> 3) - 1 - (row >> 3), -1)
+        if f == 0:
+            source, target = estimate_plane(col >> 3), row >> 3
+        else:
+            source, target = (col >> 3) - PAD, own_plane(row >> 3)
+        k = jnp.where((col & 7) == (row & 7), source - target + HALF, -1)
         hi, lo = split(fill_tap(k, taps[0], f == 1))
         kz_ref[f, pl.ds(r0, 16), 0:512] = hi
         kz_ref[f, pl.ds(r0, 16), 512:1024] = hi
@@ -117,7 +130,7 @@
 def kernel(
     bounds_ref, taps_ref, est_ref, data_ref, out_ref,
     ef, ya, rb, eb, lg, rr, newf, dv, pa, taps_v, kz, ko, kr, wx,
-    lsem, zs, zr, hs, hr, fs, fr, ys, yr, rs_s, rs_r, ag_s, ag_r,
+    lsem, zs, zr, ds, dr, ms, mr, hs, hr, fs, fr, ys, yr, rs_s, rs_r, ag_s, ag_r,
 ):
     b = lax.axis_index("block")
     v = lax.axis_index("view")
@@ -135,10 +148,14 @@
                 frm = lax.rem(vy + VIEW_Y - dy, VIEW_Y) * VIEW_X + lax.rem(vx + VIEW_X - dx, VIEW_X)
                 peers.append((to, frm))
 
-    load_est = pltpu.make_async_copy(est_ref.at[0], ef.at[0, pl.ds(PAD, Z)], lsem.at[0])
+    load_est = [
+        pltpu.make_async_copy(est_ref.at[0, m], ef.at[0, pl.ds(0, VIEWS), m], lsem.at[3 + NJ + m])
+        for m in range(PIECE)
+    ]
     load_data = pltpu.make_async_copy(data_ref.at[0, 0], dv, lsem.at[1])
     load_taps = pltpu.make_async_copy(taps_ref, taps_v, lsem.at[2])
-    load_est.start()
+    for cp in load_est:
+        cp.start()
     load_data.start()
     load_taps.start()
 
@@ -155,9 +172,8 @@
         pl.semaphore_signal(bar, inc=1, device_id={"view": to}, device_id_type=MESH)
 
     for it in range(ITERS):
-        for buf in (ef, eb):
-            buf[it, 0] = jnp.zeros((Y, X), F32)
-            buf[it, 63] = jnp.zeros((Y, X), F32)
+        eb[it, 0] = jnp.zeros((Y, X), F32)
+        eb[it, 63] = jnp.zeros((Y, X), F32)
 
         @pl.when(jnp.logical_not(has_zlo))
         def _():
@@ -167,20 +183,15 @@
         def _():
             eb[it, PAD + Z : PAD + Z + HALF] = jnp.zeros((HALF, Y, X), F32)
 
-        low = pl.ds(1, HALF) if it else pl.ds(1 + VIEWS, DIRECT)
-        high = pl.ds(PAD + Z, HALF if it else DIRECT)
-
-        @pl.when(jnp.logical_not(has_zlo))
-        def _():
-            if it == 0:
-                ef[it, 1 + v] = jnp.zeros((Y, X), F32)
-            ef[it, low] = jnp.zeros((low.size, Y, X), F32)
-
-        @pl.when(jnp.logical_not(has_zhi))
-        def _():
-            if it == 0:
-                ef[it, PAD + Z + DIRECT + v] = jnp.zeros((Y, X), F32)
-            ef[it, high] = jnp.zeros((high.size, Y, X), F32)
+        for cond, members in ((has_zhi, (0, 1)), (has_zlo, (3, 2))):
+
+            @pl.when(jnp.logical_not(cond))
+            def _():
+                for m in members:
+                    ef[it, VIEWS + v, m] = jnp.zeros((Y, X), F32)
+                if it == 0:
+                    for g in range(VIEWS):
+                        ef[it, VIEWS + g, members[0]] = jnp.zeros((Y, X), F32)
 
         for buf in (ya, rb):
 
@@ -192,47 +203,74 @@
             def _():
                 buf[it, :, PAD + Y :, :] = jnp.zeros((Z, PAD, X), F32)
 
-    load_est.wait()
+    for cp in load_est:
+        cp.wait()
     pl.semaphore_wait(bar, total)
 
-    def pair_of(buf, it, up, down, count, rows, sems, recvs, key, step):
-        one = pltpu.make_async_remote_copy(
-            src_ref=buf.at[it, pl.ds(up[0], count), rows], dst_ref=buf.at[it, pl.ds(up[1], count), rows],
-            send_sem=sems.at[(it, 0) + key], recv_sem=recvs.at[(it, 0) + key],
-            device_id={"block": b + step}, device_id_type=MESH)
-        two = pltpu.make_async_remote_copy(
-            src_ref=buf.at[it, pl.ds(down[0], count), rows], dst_ref=buf.at[it, pl.ds(down[1], count), rows],
-            send_sem=sems.at[(it, 1) + key], recv_sem=recvs.at[(it, 1) + key],
-            device_id={"block": b - step}, device_id_type=MESH)
-        return one, two
+    def z_pair(up, down, sems, recvs, key):
+        out = []
+        for d, (src, dst) in enumerate((up, down)):
+            out.append(pltpu.make_async_remote_copy(
+                src_ref=src, dst_ref=dst, send_sem=sems.at[(d,) + key], recv_sem=recvs.at[(d,) + key],
+                device_id={"block": b - BY if d else b + BY}, device_id_type=MESH))
+        return out
 
     def ratio_rims(it, j):
-        rows = pl.ds(YC * j, YC)
-        return pair_of(eb, it, (PAD + Z - HALF, 1), (PAD, PAD + Z), HALF, rows, zs, zr, (1, j), BY)
-
-    def estimate_rims(it, j):
-        rows = pl.ds(YC * j, YC)
-        return pair_of(ef, it, (PAD + Z - HALF, 1), (PAD, PAD + Z), HALF, rows, zs, zr, (0, j), BY)
+        rows = pl.ds(*CHUNKS[j])
+        return z_pair(
+            (eb.at[it, pl.ds(PAD + Z - HALF, HALF), rows], eb.at[it, pl.ds(1, HALF), rows]),
+            (eb.at[it, pl.ds(PAD, HALF), rows], eb.at[it, pl.ds(PAD + Z, HALF), rows]),
+            zs, zr, (it, j))
+
+    def middle_rims(it, part):
+        rows = pl.ds(*CHUNKS[0])
+        up = ((PAD + 24, 8, 8), (PAD + 17, 1, 7))[part]
+        down = ((PAD, PAD + Z, 8), (PAD + 8, PAD + Z + 8, 7))[part]
+        return z_pair(
+            *((eb.at[it, pl.ds(a, k), rows], eb.at[it, pl.ds(c, k), rows]) for a, c, k in (up, down)),
+            ms, mr, (it, part))
 
     def direct_rims(j):
         rows = pl.ds(FIRST_YC * j, FIRST_YC)
-        return pair_of(ef, 0, (PAD + Z - DIRECT, 1 + VIEWS), (PAD, PAD + Z), DIRECT, rows, zs, zr, (0, j), BY)
+        source, target = pl.ds(0, VIEWS), pl.ds(VIEWS, VIEWS)
+        return z_pair(
+            (ef.at[0, source, 3, rows], ef.at[0, target, 3, rows]),
+            (ef.at[0, source, 0, rows], ef.at[0, target, 0, rows]),
+            ds, dr, (j,))
 
     def shared_rims(j):
         rows = pl.ds(FIRST_YC * j, FIRST_YC)
-        return pair_of(ef, 0, (PAD + 17 + v, 1 + v), (PAD + DIRECT + v, PAD + Z + DIRECT + v), 1, rows, hs, hr, (j,), BY)
-
-    def forwards(j, w):
-        rows = pl.ds(FIRST_YC * j, FIRST_YC)
+        return z_pair(
+            (ef.at[0, v, pl.ds(2, 1), rows], ef.at[0, VIEWS + v, pl.ds(2, 1), rows]),
+            (ef.at[0, v, pl.ds(1, 1), rows], ef.at[0, VIEWS + v, pl.ds(1, 1), rows]),
+            hs, hr, (0, j))
+
+    def owned_rims(it, j):
+        rows = pl.ds(*CHUNKS[j])
+        return z_pair(
+            (newf.at[it - 1, pl.ds(2, 2), rows], ef.at[it, VIEWS + v, pl.ds(2, 2), rows]),
+            (newf.at[it - 1, pl.ds(0, 2), rows], ef.at[it, VIEWS + v, pl.ds(0, 2), rows]),
+            hs, hr, (it, j))
+
+    def forwards(it, j, outgoing):
+        rows = pl.ds(*CHUNKS[j]) if it else pl.ds(FIRST_YC * j, FIRST_YC)
+        members = pl.ds(0, 4) if it else pl.ds(1, 2)
         out = []
         for i, (to, frm) in enumerate(peers):
-            for h, first in enumerate((1, PAD + Z + DIRECT)):
-                plane = pl.ds(first + (v if w else frm), 1)
-                out.append(pltpu.make_async_remote_copy(
-                    src_ref=ef.at[0, plane, rows], dst_ref=ef.at[0, plane, rows],
-                    send_sem=fs.at[h, i, j], recv_sem=fr.at[h, i, j],
-                    device_id={"view": to}, device_id_type=MESH))
+            part = ef.at[it, VIEWS + (v if outgoing else frm), members, rows]
+            out.append(pltpu.make_async_remote_copy(
+                src_ref=part, dst_ref=part, send_sem=fs.at[it, i, j], recv_sem=fr.at[it, i, j],
+                device_id={"view": to}, device_id_type=MESH))
         return out
+
+    def forward(it, j):
+        for cp in forwards(it, j, True):
+            cp.start()
+            vsent.append(cp)
+
+    def wait_forwards(it, j):
+        for cp in forwards(it, j, False):
+            cp.wait_recv()
 
     def y_pair(buf, it, which, planes, n, c, half):
         up = pltpu.make_async_remote_copy(
@@ -335,7 +373,7 @@
         return (zpos >= bounds_ref[0, v]) & (zpos < bounds_ref[1, v])
 
     def blur_rows(it, r0, rows):
-        res = z_blur(ef[it, :, r0 : r0 + rows, :], kz[0])
+        res = z_blur(ef[it, :, :, r0 : r0 + rows, :].reshape(64, rows, X), kz[0])
         for r in range(r0, r0 + rows, 8):
             at = X * ((r - r0) // 8)
             ya[it, :, PAD + r : PAD + r + 8, :] = res[:, at : at + X].reshape(Z, 8, X)
@@ -346,17 +384,14 @@
 
     for j in FIRST:
         wait_recv(shared_rims(j), has_zlo, has_zhi)
-        for cp in forwards(j, True):
-            cp.start()
-            vsent.append(cp)
+        forward(0, j)
     build_xy(taps, ko, kr, wx, 0)
     build_xy(taps, ko, kr, wx, 1)
     build_z(taps, kz, 1)
     load_data.wait()
     for j in FIRST:
         wait_recv(direct_rims(j), has_zlo, has_zhi)
-        for cp in forwards(j, False):
-            cp.wait_recv()
+        wait_forwards(0, j)
         blur_rows(0, FIRST_YC * j, FIRST_YC)
 
     for it in range(ITERS):
@@ -371,7 +406,7 @@
         def rims(buf, p):
             return jnp.concatenate([buf[it, p, 0:PAD], buf[it, p, PAD + Y :]], axis=0)
 
-        for c in range(NZC):
+        for c in ZORDER:
             span = range(ZC * c, ZC * (c + 1), 2)
             parts = []
             for p in span:
@@ -387,14 +422,13 @@
                 res = y_blur([rb[it, p, own], rb[it, p + 1, own]], ko[1][:, :144])
                 eb[it, PAD + p] = res[:, :X]
                 eb[it, PAD + p + 1] = res[:, X:]
-            if c == NZC // 2 - 1:
-                for j in ORDER[:2]:
-                    pair = ratio_rims(it, j)
-                    zsent.append(pair)
-                    start_down(pair)
-        for j in ORDER[:2]:
-            start_up(ratio_rims(it, j))
-        for c in range(NZC):
+            pair = middle_rims(it, 0 if c in (0, 3) else 1)
+            if c < NZC // 2:
+                start_down(pair)
+                zsent.append(pair)
+            else:
+                start_up(pair)
+        for c in ZORDER:
             wait_recv(ratio_y_rims(it, c), has_ylo, has_yhi)
             for p in range(ZC * c, ZC * (c + 1), 2):
                 res = y_blur([rims(rb, p), rims(rb, p + 1)], kr[1][:, :96])
@@ -402,26 +436,31 @@
                     edge = res[:, X * h : X * (h + 1)]
                     eb[it, PAD + p + h, 0:PAD] += edge[:PAD]
                     eb[it, PAD + p + h, 2 * PAD :] += edge[PAD:]
-            if c == NZC // 2 - 1:
-                for j in ORDER[2:]:
+            if c == ZORDER[2]:
+                for j in range(1, NJ):
                     pair = ratio_rims(it, j)
                     zsent.append(pair)
                     start_down(pair)
-        for j in ORDER[2:]:
+        for j in range(1, NJ):
             start_up(ratio_rims(it, j))
 
         mine = v * PIECE
 
         def log_step(j):
-            wait_recv(ratio_rims(it, j), has_zlo, has_zhi)
-            res = z_blur(eb[it, :, YC * j : YC * (j + 1), :], kz[1])
-            for g in range(YC // 8):
-                r0 = YC * j + 8 * g
+            if j:
+                wait_recv(ratio_rims(it, j), has_zlo, has_zhi)
+            else:
+                for part in range(2):
+                    wait_recv(middle_rims(it, part), has_zlo, has_zhi)
+            r0, n = CHUNKS[j]
+            res = z_blur(eb[it, :, r0 : r0 + n, :], kz[1])
+            for g in range(n // 8):
+                r = r0 + 8 * g
                 logs = jnp.log(res[:, X * g : X * (g + 1)].reshape(Z, 8, X))
                 for p in range(Z):
-                    keep = jnp.where(own_z(p), own_y[r0 : r0 + 8], 0.0)
-                    lg[it, p, r0 : r0 + 8, :] = keep * logs[p]
-            rows = pl.ds(YC * j, YC)
+                    keep = jnp.where(own_z(own_plane(p)), own_y[r : r + 8], 0.0)
+                    lg[it, p, r : r + 8, :] = keep * logs[p]
+            rows = pl.ds(*CHUNKS[j])
             for i, (to, frm) in enumerate(peers):
                 cp = pltpu.make_async_remote_copy(
                     src_ref=lg.at[it, pl.ds(to * PIECE, PIECE), rows],
@@ -432,34 +471,36 @@
                 vsent.append(cp)
 
         def sum_step(j):
-            rows = pl.ds(YC * j, YC)
-            acc = lg[it, pl.ds(mine, PIECE), YC * j : YC * (j + 1), :]
+            rows = pl.ds(*CHUNKS[j])
+            r0, n = CHUNKS[j]
+            acc = lg[it, pl.ds(mine, PIECE), r0 : r0 + n, :]
             for i in range(VIEWS - 1):
                 pltpu.make_async_remote_copy(
                     src_ref=lg.at[it, pl.ds(0, PIECE), rows], dst_ref=rr.at[it, i, :, rows],
                     send_sem=rs_s.at[it, i, j], recv_sem=rs_r.at[it, i, j],
                     device_id={"view": peers[i][0]}, device_id_type=MESH).wait_recv()
-                acc = acc + rr[it, i, :, YC * j : YC * (j + 1), :]
-            yj = ypos[YC * j : YC * (j + 1)]
+                acc = acc + rr[it, i, :, r0 : r0 + n, :]
+            yj = ypos[r0 : r0 + n]
             ins = [
                 jnp.where((yj >= bounds_ref[2, w]) & (yj < bounds_ref[3, w]), 1.0, 0.0).astype(F32)
                 for w in range(VIEWS)
             ]
             for p in range(PIECE):
-                zpos = z0 + mine + p
-                count = jnp.zeros((YC, X), F32)
+                zpos = z0 + v + VIEWS * p
+                count = jnp.zeros((n, X), F32)
                 for w in range(VIEWS):
                     inz = (zpos >= bounds_ref[0, w]) & (zpos < bounds_ref[1, w])
                     count = count + jnp.where(inz, ins[w], 0.0)
-                old = ef[it, PAD + mine + p, YC * j : YC * (j + 1), :]
+                old = ef[it, v, p, r0 : r0 + n, :]
                 new = old * jnp.exp(acc[p] / count)
-                newf[it, p, YC * j : YC * (j + 1), :] = new
+                newf[it, p, r0 : r0 + n, :] = new
                 if it < ITERS - 1:
-                    ef[it + 1, PAD + mine + p, YC * j : YC * (j + 1), :] = new
+                    ef[it + 1, v, p, r0 : r0 + n, :] = new
             if it < ITERS - 1:
-                target = ef.at[it + 1, pl.ds(PAD + mine, PIECE), rows]
+                target = ef.at[it + 1, v, :, rows]
+                send_z(owned_rims(it + 1, j))
             else:
-                target = out_ref.at[0, pl.ds(mine, PIECE), rows]
+                target = out_ref.at[0, :, v, rows]
                 cp = pltpu.make_async_copy(newf.at[it, :, rows], target, lsem.at[3 + j])
                 cp.start()
                 vsent.append(cp)
@@ -472,30 +513,35 @@
                 vsent.append(cp)
 
         def gather_step(j):
-            rows = pl.ds(YC * j, YC)
+            rows = pl.ds(*CHUNKS[j])
             for i, (to, frm) in enumerate(peers):
                 if it < ITERS - 1:
-                    target = ef.at[it + 1, pl.ds(PAD + frm * PIECE, PIECE), rows]
+                    target = ef.at[it + 1, frm, :, rows]
                 else:
-                    target = out_ref.at[0, pl.ds(frm * PIECE, PIECE), rows]
+                    target = out_ref.at[0, :, frm, rows]
                 pltpu.make_async_remote_copy(
                     src_ref=newf.at[it, :, rows], dst_ref=target,
                     send_sem=ag_s.at[it, i, j], recv_sem=ag_r.at[it, i, j],
                     device_id={"view": to}, device_id_type=MESH).wait_recv()
+
+        for n in range(NJ + S3):
+            if n < NJ:
+                log_step(n)
+            if 0 <= n - S1 < NJ:
+                sum_step(n - S1)
             if it < ITERS - 1:
-                send_z(estimate_rims(it + 1, j))
-
-        for n in range(NJ + 6):
-            if n < NJ:
-                log_step(ORDER[n])
-            if 0 <= n - 2 < NJ:
-                sum_step(ORDER[n - 2])
-            if 0 <= n - 4 < NJ:
-                gather_step(ORDER[n - 4])
-            if 0 <= n - 6 < NJ and it < ITERS - 1:
-                j = ORDER[n - 6]
-                wait_recv(estimate_rims(it + 1, j), has_zlo, has_zhi)
-                blur_rows(it + 1, YC * j, YC)
+                if 0 <= n - S2 < NJ:
+                    j = n - S2
+                    wait_recv(owned_rims(it + 1, j), has_zlo, has_zhi)
+                    forward(it + 1, j)
+                if 0 <= n - S3 < NJ:
+                    j = n - S3
+                    gather_step(j)
+                    wait_forwards(it + 1, j)
+                    blur_rows(it + 1, *CHUNKS[j])
+        if it == ITERS - 1:
+            for j in range(NJ):
+                gather_step(j)
 
     for pair in zsent:
         wait_send(pair, has_zlo, has_zhi)
@@ -516,16 +562,16 @@
     dma = pltpu.SemaphoreType.DMA
     return pl.pallas_call(
         kernel,
-        out_shape=jax.ShapeDtypeStruct(estimate.shape, F32),
+        out_shape=pltpu.VMEM((1, PIECE, VIEWS, Y, X), F32),
         in_specs=[
             pl.BlockSpec(memory_space=pltpu.SMEM),
             pl.BlockSpec(memory_space=pltpu.HBM),
             pl.BlockSpec(memory_space=pltpu.HBM),
             pl.BlockSpec(memory_space=pltpu.HBM),
         ],
-        out_specs=pl.BlockSpec(memory_space=pl.ANY),
+        out_specs=pl.BlockSpec(memory_space=pltpu.VMEM),
         scratch_shapes=[
-            pltpu.VMEM((ITERS, 64, Y, X), F32),
+            pltpu.VMEM((ITERS, 16, PIECE, Y, X), F32),
             pltpu.VMEM((ITERS, Z, 80, X), F32),
             pltpu.VMEM((ITERS, Z, 80, X), F32),
             pltpu.VMEM((ITERS, 64, Y, X), F32),
@@ -539,13 +585,17 @@
             pltpu.VMEM((2, Y, 256), BF16),
             pltpu.VMEM((2, 2 * PAD, 128), BF16),
             pltpu.VMEM((2, 256, 256), BF16),
-            dma((3 + NJ,)),
-            dma((ITERS, 2, 2, NJ)),
-            dma((ITERS, 2, 2, NJ)),
-            dma((1, 2, FIRST_NJ)),
-            dma((1, 2, FIRST_NJ)),
-            dma((2, VIEWS - 1, FIRST_NJ)),
-            dma((2, VIEWS - 1, FIRST_NJ)),
+            dma((3 + NJ + PIECE,)),
+            dma((2, ITERS, NJ)),
+            dma((2, ITERS, NJ)),
+            dma((2, FIRST_NJ)),
+            dma((2, FIRST_NJ)),
+            dma((2, ITERS, 2)),
+            dma((2, ITERS, 2)),
+            dma((2, ITERS, NJ)),
+            dma((2, ITERS, NJ)),
+            dma((ITERS, VIEWS - 1, NJ)),
+            dma((ITERS, VIEWS - 1, NJ)),
             dma((ITERS, 2, 2, NZC)),
             dma((ITERS, 2, 2, NZC)),
             dma((ITERS, VIEWS - 1, NJ)),
@@ -554,10 +604,10 @@
             dma((ITERS, VIEWS - 1, NJ)),
         ],
         compiler_params=pltpu.CompilerParams(
-            collective_id=0, has_side_effects=True, vmem_limit_bytes=64000000
+            collective_id=0, has_side_effects=True, vmem_limit_bytes=60000000
         ),
         name="deconvolve",
-    )(view_bounds.T, psf_taps.transpose(1, 0, 2), estimate, views_data)
+    )(view_bounds.T, psf_taps.transpose(1, 0, 2), estimate.reshape(1, PIECE, VIEWS, Y, X), views_data).reshape(estimate.shape)
 
 
 def solution(mesh):

time: 127 us -> 121 us (0.953)
  the two profiles are of different devices: /device:TPU:96 before, /device:TPU:1 now
where the time goes in v3:
time: 121 us; the launch traced here: 120 us
  Pallas kernels  120 us (99%)
    pallas_call x1, Pallas kernels, body(): pl.pallas_call(kernel, out_shape=pltpu.VMEM((1, PIECE, VIEWS, Y, X), F32)...  120 us

profile of v3, /device:TPU:1, one launch (start us, length us, event | category | flops | bytes accessed | tf_op | source)
XLA Modules:
  0.0 120.5 jit_solution(17920346759408473593)
XLA Ops:
  0.0 119.6 %deconvolve.1 = f32[1,4,8,48,128]{4,3,2,1,0:T(8,128)S(1)} custom-call(s32[4,8]{1,0:T(4,128)} %bitcast.6, f32[3,1,31]{2,1,0:T(1,128)} %bitcast.7, f32[1,4,8,48,128]{4,3,2,1,0:T(8,128)} %bitcast.5, f32[1,1,32,48,128]{4,3,2,1,0:T(8,128)} %data_ref.1), custom_call_target="tpu_custom_call" | custom-call | tf_op jit(solution)/shard_map/deconvolve/pallas_call | solution.py:563
  119.6 0.9 copy.6

commit v4 on v3

--- a/solution.py
+++ b/solution.py
@@ -20,12 +20,14 @@
 VIEW_X, VIEW_Y = 4, 2
 VIEWS = VIEW_X * VIEW_Y
 PIECE = Z // VIEWS
-CHUNKS = ((16, 16), (0, 16), (32, 8), (40, 8))
+CHUNKS = ((16, 8), (24, 8), (0, 16), (32, 8), (40, 8))
+MIDDLE = 2
+PROC = ((0, 2, 3, 4, 1), (0, 1, 2, 3, 4))
 NJ = len(CHUNKS)
 FIRST_YC = 16
 FIRST_NJ = Y // FIRST_YC
 FIRST = (0, 2, 1)
-S1, S2, S3 = 3, 5, 7
+S1, S2, S3 = 4, 7, 9
 ZC = 8
 NZC = Z // ZC
 ZORDER = (0, 3, 1, 2)
@@ -223,7 +225,7 @@
             zs, zr, (it, j))
 
     def middle_rims(it, part):
-        rows = pl.ds(*CHUNKS[0])
+        rows = pl.ds(16, 16)
         up = ((PAD + 24, 8, 8), (PAD + 17, 1, 7))[part]
         down = ((PAD, PAD + Z, 8), (PAD + 8, PAD + Z + 8, 7))[part]
         return z_pair(
@@ -437,19 +439,19 @@
                     eb[it, PAD + p + h, 0:PAD] += edge[:PAD]
                     eb[it, PAD + p + h, 2 * PAD :] += edge[PAD:]
             if c == ZORDER[2]:
-                for j in range(1, NJ):
+                for j in range(MIDDLE, NJ):
                     pair = ratio_rims(it, j)
                     zsent.append(pair)
                     start_down(pair)
-        for j in range(1, NJ):
+        for j in range(MIDDLE, NJ):
             start_up(ratio_rims(it, j))
 
         mine = v * PIECE
 
         def log_step(j):
-            if j:
+            if j >= MIDDLE:
                 wait_recv(ratio_rims(it, j), has_zlo, has_zhi)
-            else:
+            elif j == 0:
                 for part in range(2):
                     wait_recv(middle_rims(it, part), has_zlo, has_zhi)
             r0, n = CHUNKS[j]
@@ -526,21 +528,21 @@
 
         for n in range(NJ + S3):
             if n < NJ:
-                log_step(n)
+                log_step(PROC[it][n])
             if 0 <= n - S1 < NJ:
-                sum_step(n - S1)
+                sum_step(PROC[it][n - S1])
             if it < ITERS - 1:
                 if 0 <= n - S2 < NJ:
-                    j = n - S2
+                    j = PROC[it][n - S2]
                     wait_recv(owned_rims(it + 1, j), has_zlo, has_zhi)
                     forward(it + 1, j)
                 if 0 <= n - S3 < NJ:
-                    j = n - S3
+                    j = PROC[it][n - S3]
                     gather_step(j)
                     wait_forwards(it + 1, j)
                     blur_rows(it + 1, *CHUNKS[j])
         if it == ITERS - 1:
-            for j in range(NJ):
+            for j in PROC[it]:
                 gather_step(j)
 
     for pair in zsent:

time: 121 us -> 120 us (level)
  Pallas kernels: 120 us -> 118 us
    pallas_call x1, Pallas kernels: 120 us -> 118 us  [body(): pl.pallas_call(kernel, out_shape=pltpu.VMEM((1, PIECE, VIEWS, Y, X), F32)...]
where the time goes in v4:
time: 120 us; the launch traced here: 119 us
  Pallas kernels  118 us (98%)
    pallas_call x1, Pallas kernels, body(): pl.pallas_call(kernel, out_shape=pltpu.VMEM((1, PIECE, VIEWS, Y, X), F32)...  118 us

profile of v4, /device:TPU:1, one launch (start us, length us, event | category | flops | bytes accessed | tf_op | source)
XLA Modules:
  0.0 119.2 jit_solution(2776900158348982502)
XLA Ops:
  0.0 118.3 %deconvolve.1 = f32[1,4,8,48,128]{4,3,2,1,0:T(8,128)S(1)} custom-call(s32[4,8]{1,0:T(4,128)} %bitcast.6, f32[3,1,31]{2,1,0:T(1,128)} %bitcast.7, f32[1,4,8,48,128]{4,3,2,1,0:T(8,128)} %bitcast.5, f32[1,1,32,48,128]{4,3,2,1,0:T(8,128)} %data_ref.1), custom_call_target="tpu_custom_call" | custom-call | tf_op jit(solution)/shard_map/deconvolve/pallas_call | solution.py:565
  118.4 0.9 copy.6

commit v5 on v4

--- a/solution.py
+++ b/solution.py
@@ -28,6 +28,7 @@
 FIRST_NJ = Y // FIRST_YC
 FIRST = (0, 2, 1)
 S1, S2, S3 = 4, 7, 9
+S1_LAST = 2
 ZC = 8
 NZC = Z // ZC
 ZORDER = (0, 3, 1, 2)
@@ -529,8 +530,9 @@
         for n in range(NJ + S3):
             if n < NJ:
                 log_step(PROC[it][n])
-            if 0 <= n - S1 < NJ:
-                sum_step(PROC[it][n - S1])
+            late = S1 if it < ITERS - 1 else S1_LAST
+            if 0 <= n - late < NJ:
+                sum_step(PROC[it][n - late])
             if it < ITERS - 1:
                 if 0 <= n - S2 < NJ:
                     j = PROC[it][n - S2]

time: 120 us -> 124 us (1.033)
  Pallas kernels: 118 us -> 123 us
    pallas_call x1, Pallas kernels: 118 us -> 123 us  [body(): pl.pallas_call(kernel, out_shape=pltpu.VMEM((1, PIECE, VIEWS, Y, X), F32)...]
where the time goes in v5:
time: 124 us
  Pallas kernels  123 us (99%)
    pallas_call x1, Pallas kernels, body(): pl.pallas_call(kernel, out_shape=pltpu.VMEM((1, PIECE, VIEWS, Y, X), F32)...  123 us

profile of v5, /device:TPU:1, one launch (start us, length us, event | category | flops | bytes accessed | tf_op | source)
XLA Modules:
  0.0 124.1 jit_solution(8191711887708359997)
XLA Ops:
  0.0 123.2 %deconvolve.1 = f32[1,4,8,48,128]{4,3,2,1,0:T(8,128)S(1)} custom-call(s32[4,8]{1,0:T(4,128)} %bitcast.6, f32[3,1,31]{2,1,0:T(1,128)} %bitcast.7, f32[1,4,8,48,128]{4,3,2,1,0:T(8,128)} %bitcast.5, f32[1,1,32,48,128]{4,3,2,1,0:T(8,128)} %data_ref.1), custom_call_target="tpu_custom_call" | custom-call | tf_op jit(solution)/shard_map/deconvolve/pallas_call | solution.py:567
  123.2 0.9 copy.6
